TPU v7x, 32 devices: a whole 2x2x4 slice. The times are simulated.
32 devices in a mesh: jobs: 2 (over x), clus: 16 (over z, y, core).
Axes of the slice: x: 2, y: 2, z: 4, core: 2. Of those that a mesh axis runs over, the one named last changes fastest.
Arguments:
- vertices: float32 [3, 65536], P(None, ('jobs', 'clus')), parts along dimension 1, may hold values from 0 to 17
- panel_vertices: int32 [3, 131072], P(None, ('jobs', 'clus')), parts along dimension 1, may hold values from 0 to 32767, as said below
- near_pairs: int32 [512, 4], P(('jobs', 'clus')), parts along dimension 0, may hold values from -1 to 255, as said below
- far_pairs: int32 [512, 32], P(('jobs', 'clus')), parts along dimension 0, may hold values from 0 to 255, as said below
- basis: float32 [32, 131072], P(None, ('jobs', 'clus')), parts along dimension 1, may hold values from -0.75 to 0.75
- krylov: float32 [16, 131072], P(None, ('jobs', 'clus')), parts along dimension 1, may hold values from -12 to 12
Outputs:
- next_basis: float32 [16, 131072], P(None, ('jobs', 'clus')), parts along dimension 1
- second_image: float32 [16, 131072], P(None, ('jobs', 'clus')), parts along dimension 1
There are 2 independent parts, one for each index of `jobs`. A program takes and returns all parts, laid end to end along the dimension named above; each array names one. Nothing has to cross between parts.
Inputs may be any that keep to these rules, and one draw needn't show every extreme that they name: `panel_vertices`: the vertices of a panel of cluster c are among vertices c * 128 to (c + 1) * 128 - 1. `near_pairs`: row c starts with c itself, then distinct clusters j with |j // 16 - c // 16| <= 1; live entries come first and -1 fills the rest; some row has all 4 slots live. `far_pairs`: row c holds 32 distinct clusters j with 2 <= |j // 16 - c // 16| <= 4.
All inputs are finite; a program needn't handle non-finite values.
Results may differ from a plain program's by a relative error of at most 0.0003.
Values sent between devices are 32-bit elements; how exact they have to be, the bound alone decides.
No kernel may reach another device: no remote copies, remote signals or barrier semaphores. Data moves between devices by JAX's collectives and lax.ppermute only.
A program may use at most 128 MiB of HBM per device.

v0:
```python
import jax
import jax.numpy as jnp
from jax import lax
from jax.sharding import PartitionSpec as P

REACH = 4


SMOOTHING = 0.04
COULOMB = 2.0
PROXY_RADIUS = 0.6
HIGHEST_PRECISION = lax.Precision.HIGHEST


def from_behind(value, axis, steps):
    count = lax.axis_size(axis)
    first, last = (max(0, -steps), min(count, count - steps))
    return lax.ppermute(value, axis, [(source, source + steps) for source in range(first, last)])


def extended_2(cells, sides, width):
    for axis, dim in sides:
        count = lax.axis_size(axis)
        ends = count - 1
        head = lax.slice_in_dim(cells, 0, width, axis=dim)
        tail = lax.slice_in_dim(cells, cells.shape[dim] - width, cells.shape[dim], axis=dim)
        cells = jnp.concatenate(
            [
                lax.ppermute(tail, axis, [(i, (i + 1) % count) for i in range(ends)]),
                cells,
                lax.ppermute(head, axis, [((i + 1) % count, i) for i in range(ends)]),
            ],
            axis=dim,
        )
    return cells


def proxy_directions(points):
    counter = jnp.arange(points).astype(jnp.float32)
    height = 1.0 - (2.0 * counter + 1.0) / points
    radial = jnp.sqrt(1.0 - height * height)
    azimuth = counter * 2.399963
    return jnp.stack([radial * jnp.cos(azimuth), radial * jnp.sin(azimuth), height])


def geometry(vertices, corner_index):
    corners = vertices[:, corner_index]
    centroid = (corners[:, 0] + corners[:, 1] + corners[:, 2]) / 3.0
    edge_one = corners[:, 1] - corners[:, 0]
    edge_two = corners[:, 2] - corners[:, 0]
    normal = jnp.stack(
        [
            edge_one[1] * edge_two[2] - edge_one[2] * edge_two[1],
            edge_one[2] * edge_two[0] - edge_one[0] * edge_two[2],
            edge_one[0] * edge_two[1] - edge_one[1] * edge_two[0],
        ]
    )
    panel_area = 0.5 * jnp.sqrt(jnp.sum(normal * normal, axis=0))
    return (centroid, panel_area)


def near_term(target, source, charges, live_mask):
    offsets = target[:, :, :, None] - source[:, :, None, :]
    kernel = 1.0 / jnp.sqrt(jnp.sum(offsets * offsets, axis=0) + SMOOTHING)
    masked = charges * live_mask[None, :, None]
    return jnp.einsum("cpq,rcq->rcp", kernel, masked, precision=HIGHEST_PRECISION)


def coupling(target_proxy, source_proxy):
    offsets = target_proxy[:, :, None, :, None] - source_proxy[:, :, :, None, :]
    return 1.0 / jnp.sqrt(jnp.sum(offsets * offsets, axis=0) + SMOOTHING)


def near_sum(target, source_centroid, source_charges, local_pairs):
    running = jnp.zeros((source_charges.shape[0], target.shape[1], target.shape[2]), jnp.float32)
    for slot_index in range(local_pairs.shape[1]):
        column = local_pairs[:, slot_index]
        chosen = jnp.maximum(column, 0)
        running = running + near_term(
            target,
            source_centroid[:, chosen],
            source_charges[:, chosen],
            (column >= 0).astype(jnp.float32),
        )
    return running


def cluster_window(cluster_table, clusters_here, position):
    pieces = []
    for offset in range(-REACH, REACH + 1):
        if offset == 0:
            pieces.append(cluster_table)
        elif abs(offset) == 1:
            pieces.append(jnp.zeros_like(cluster_table))
        else:
            pieces.append(from_behind(cluster_table, "clus", -offset))
    return (jnp.concatenate(pieces, axis=1), (position - REACH) * clusters_here)


def far_part(coupler, moment_table, far_local, basis_blocks, conductors, factor_rank):
    window_span = moment_table.shape[1]
    selected = moment_table.reshape(conductors, factor_rank, window_span)[:, :, far_local]
    far_field = jnp.einsum("cfab,rbcf->rca", coupler, selected, precision=HIGHEST_PRECISION)
    return jnp.einsum("acp,rca->rcp", basis_blocks, far_field, precision=HIGHEST_PRECISION)


def body(vertices, panel_vertices, near_pairs, far_pairs, basis, krylov):
    clusters_here = near_pairs.shape[0]
    conductors = krylov.shape[0]
    panels_here = krylov.shape[1]
    factor_rank = basis.shape[0]
    panel_width = panels_here // clusters_here
    position = lax.axis_index("clus")
    devices = lax.axis_size("clus")
    centroid, panel_area = geometry(vertices, panel_vertices - position * vertices.shape[1])
    own_centroid = centroid.reshape(3, clusters_here, panel_width)
    centers = jnp.mean(own_centroid, axis=2)
    area_blocks = panel_area.reshape(clusters_here, panel_width)
    basis_blocks = basis.reshape(factor_rank, clusters_here, panel_width)
    directions = proxy_directions(factor_rank)
    near_local = jnp.where(near_pairs >= 0, near_pairs - (position - 1) * clusters_here, -1)
    moment_rows = conductors * factor_rank

    def project(weighted):
        blocks = weighted.reshape(conductors, clusters_here, panel_width)
        moments = jnp.einsum("acp,rcp->rac", basis_blocks, blocks, precision=HIGHEST_PRECISION)
        return moments.reshape(moment_rows, clusters_here)

    weighted = panel_area[None, :] * krylov
    extended = extended_2(
        jnp.concatenate([centroid, weighted], axis=0), (("clus", 1),), panels_here
    )
    source_centroid = extended[:3].reshape(3, 3 * clusters_here, panel_width)
    source_charges = extended[3:].reshape(conductors, 3 * clusters_here, panel_width)
    cluster_table, anchor = cluster_window(
        jnp.concatenate([project(weighted), centers], axis=0), clusters_here, position
    )
    far_local = far_pairs - anchor
    source_centers = cluster_table[moment_rows:][:, far_local]
    target_proxy = centers[:, :, None] + PROXY_RADIUS * directions[:, None, :]
    source_proxy = source_centers[:, :, :, None] + PROXY_RADIUS * directions[:, None, None, :]
    coupler = coupling(target_proxy, source_proxy)
    near_part = near_sum(own_centroid, source_centroid, source_charges, near_local)
    far_potential = far_part(
        coupler, cluster_table[:moment_rows], far_local, basis_blocks, conductors, factor_rank
    )
    image = (COULOMB * area_blocks[None] * (near_part + far_potential)).reshape(
        conductors, panels_here
    )
    correlation, squared = lax.psum(
        (jnp.sum(krylov * image, axis=1), jnp.sum(krylov * krylov, axis=1)), "clus"
    )
    projection = correlation / (squared + 1e-06)
    residual = image - projection[:, None] * krylov
    energy = lax.psum(jnp.sum(residual * residual, axis=1), "clus")
    scaling = jnp.sqrt(energy / (panels_here * devices) + 1e-06)
    next_basis = residual / scaling[:, None]
    weighted = panel_area[None, :] * next_basis
    extended = extended_2(weighted, (("clus", 1),), panels_here)
    source_charges = extended.reshape(conductors, 3 * clusters_here, panel_width)
    moment_table, anchor = cluster_window(project(weighted), clusters_here, position)
    far_local = far_pairs - anchor
    near_part = near_sum(own_centroid, source_centroid, source_charges, near_local)
    far_potential = far_part(
        coupler, moment_table, far_local, basis_blocks, conductors, factor_rank
    )
    second_image = (COULOMB * area_blocks[None] * (near_part + far_potential)).reshape(
        conductors, panels_here
    )
    return (next_basis, second_image)


def solution(mesh):
    return jax.shard_map(
        body,
        mesh=mesh,
        in_specs=(
            P(None, ("jobs", "clus")),
            P(None, ("jobs", "clus")),
            P(("jobs", "clus"), None),
            P(("jobs", "clus"), None),
            P(None, ("jobs", "clus")),
            P(None, ("jobs", "clus")),
        ),
        out_specs=(P(None, ("jobs", "clus")), P(None, ("jobs", "clus"))),
        check_vma=False,
    )
```

profile of v0, /device:TPU:13, one launch (start us, length us, event | category | flops | bytes accessed | tf_op | source)
XLA Modules:
  0.0 269.9 jit_solution(18340943274468916322)
XLA Ops:
  0.6 0.9 compare_select_fusion
  1.6 1.1 copy.158
  2.7 41.3 %gather_fusion = f32[12288,3]{1,0:T(8,128)} fusion(f32[3,2048]{0,1:T(8,128)S(1)} %copy.158, s32[12288]{0:T(1024)S(1)} %broadcast_clamp_fusion), kind=kCustom, calls=%fused_computation | custom fusion | bytes 344064 | tf_op jit(solution)/shard_map/gather | solution.py:47
  44.0 4.5 %copy.159 = f32[3,4096,3]{1,2,0:T(4,128)S(1)} copy(f32[3,4096,3]{2,1,0:T(8,128)} %bitcast.151) | data formatting | bytes 294912 | tf_op jit(solution)/shard_map/gather | solution.py:47
  49.0 0.5 copy-done.11
  49.6 0.5 convolution_bitcast_fusion.1
  50.2 2.1 collective-permute-start.7
  52.3 2.5 collective-permute-start.6
  54.9 2.4 collective-permute-start.5
  57.3 4.0 %collective-permute-start.4 = (f32[515,16]{0,1:T(8,128)S(1)}, f32[515,16]{0,1:T(8,128)S(1)}, u32[]{:S(2)}, u32[]{:S(2)}) collective-permute-start(f32[515,16]{0,1:T(8,128)S(1)} %pad_maximum_fusion.4), channel_id=1, source_target_pairs={{0,2},{1,3},{2,4},{3,5},{4,6},{5,7},{6,8},{7,9},{8,10},{9,11},{10,... | collective-permute-start | bytes 98888 | tf_op jit(solution)/shard_map/ppermute | solution.py:18
  61.3 3.4 %collective-permute-start.2 = (f32[515,16]{0,1:T(8,128)S(1)}, f32[515,16]{0,1:T(8,128)S(1)}, u32[]{:S(2)}, u32[]{:S(2)}) collective-permute-start(f32[515,16]{0,1:T(8,128)S(1)} %pad_maximum_fusion.4), channel_id=1, source_target_pairs={{0,4},{1,5},{2,6},{3,7},{4,8},{5,9},{6,10},{7,11},{8,12},{9,13},{1... | collective-permute-start | bytes 98888 | tf_op jit(solution)/shard_map/ppermute | solution.py:18
  64.8 0.6 fusion.77
  65.6 0.8 pad_maximum_fusion.2
  66.4 0.6 sqrt.62
  67.1 3.9 %collective-permute-start.3 = (f32[515,16]{0,1:T(8,128)S(1)}, f32[515,16]{0,1:T(8,128)S(1)}, u32[]{:S(2)}, u32[]{:S(2)}) collective-permute-start(f32[515,16]{0,1:T(8,128)S(1)} %pad_maximum_fusion.4), channel_id=1, source_target_pairs={{0,3},{1,4},{2,5},{3,6},{4,7},{5,8},{6,9},{7,10},{8,11},{9,12},{10... | collective-permute-start | bytes 98888 | tf_op jit(solution)/shard_map/ppermute | solution.py:18
  71.0 1.7 collective-permute-done.3
  72.7 2.7 collective-permute-start.1
  75.4 4.0 %collective-permute-start = (f32[19,4096]{1,0:T(8,128)}, f32[19,4096]{1,0:T(8,128)}, u32[]{:S(2)}, u32[]{:S(2)}) collective-permute-start(f32[19,4096]{1,0:T(8,128)} %pad_maximum_fusion.2), channel_id=1, source_target_pairs={{0,1},{1,2},{2,3},{3,4},{4,5},{5,6},{6,7},{7,8},{8,9},{9,10},{10,1... | collective-permute-start | bytes 933896 | tf_op jit(solution)/shard_map/ppermute | solution.py:29
  79.5 1.0 gather_fusion.10
  81.0 0.6 copy.172
  81.6 1.2 broadcast_add_fusion
  82.8 3.1 %gather_fusion.9 = f32[512,16,32]{2,1,0:T(8,128)} fusion(f32[16,32,144]{1,0,2:T(8,128)S(1)} %copy.172, s32[1024]{0:T(1024)S(1)} %pad_clamp_fusion), kind=kCustom, calls=%fused_computation.9 | custom fusion | bytes 2099200 | tf_op jit(solution)/shard_map/gather | solution.py:102
  85.9 9.7 %multiply_reduce_fusion = f32[16,32,32,32]{3,2,1,0:T(8,128)} fusion(f32[3,16,32,32]{3,2,1,0:T(8,128)} %broadcast_add_fusion, f32[3,16,32]{2,1,0:T(8,128)S(1)} %broadcast_add_fusion.1), kind=kLoop, calls=%fused_computation.16 | loop fusion | flops 4194304 | bytes 2299904 | tf_op jit(solution)/shard_map/reduce_sum | solution.py:71
  95.6 10.7 %fusion.32 = f32[16,16,32]{2,0,1:T(8,128)S(1)} fusion(f32[16,32,16,32]{1,0,3,2:T(8,128)S(1)} %bitcast.145, f32[16,32,32,32]{3,2,1,0:T(8,128)} %multiply_reduce_fusion), kind=kOutput, calls=%fused_computation.59 | convolution fusion | flops 101187584 | bytes 3178496 | tf_op jit(solution)/shard_map/cfab,rbcf->rca/dot_general | solution.py:103
  106.3 1.1 fusion.37
  107.4 0.9 pad_maximum_fusion.3
  108.4 0.6 gather_fusion.8
  109.0 0.6 gather_fusion.6
  109.6 1.1 pad_maximum_fusion
  110.8 1.3 gather_fusion.7
  112.1 0.6 gather_fusion.5
  112.7 0.6 gather_fusion.4
  113.3 0.6 gather_fusion.3
  113.9 0.6 gather_fusion.2
  114.5 1.3 gather_fusion.1
  115.8 0.6 copy.163
  116.4 11.4 %multiply_reduce_fusion.1 = (f32[16,256,256]{2,1,0:T(8,128)}, f32[16,256,256]{2,1,0:T(8,128)S(1)}, f32[16,256,256]{2,1,0:T(8,128)S(1)}, f32[16,256,256]{2,1,0:T(8,128)}) fusion(f32[3,16,256]{2,1,0:T(8,128)S(1)} %copy.167, f32[3,16,256]{2,1,0:T(8,128)S(1)} %get-tuple-element.13, f32[3,16,256]{2,1,0:T(8,128)} %copy.163, f32[3,16,256]{2,1,0:T(8,128)S(1)} %copy.165, ...), kind=kLoop, calls=%fused_computation.17 | loop fusion | flops 33554432 | bytes 17022976 | tf_op jit(solution)/shard_map/reduce_sum | solution.py:64
  127.9 8.7 %fusion.5 = f32[16,16,256]{2,1,0:T(8,128)S(1)} fusion(f32[16,256,256]{2,1,0:T(8,128)} %get-tuple-element.7, f32[16,16,256]{2,1,0:T(8,128)} %gather_fusion.1, f32[16]{0:T(128)} %get-tuple-element.23), kind=kOutput, calls=%fused_computation.31 | convolution fusion | flops 202440704 | bytes 4718656 | tf_op jit(solution)/shard_map/cpq,rcq->rcp/dot_general | solution.py:66
  136.6 3.5 %fusion.30 = f32[16,16,256]{2,1,0:T(8,128)S(1)} fusion(f32[16,16,256]{2,1,0:T(8,128)S(1)} %fusion.5, f32[16,256,256]{2,1,0:T(8,128)S(1)} %get-tuple-element.5, f32[16,16,256]{2,1,0:T(8,128)S(1)} %gather_fusion.3, f32[16]{0:T(128)S(1)} %copy-done.19), kind=kOutput, calls=%fused_computation.57 | convolution fusion | flops 202506240 | bytes 4980800 | tf_op jit(solution)/shard_map/cpq,rcq->rcp/dot_general | solution.py:66
  140.2 3.5 %fusion.28 = f32[16,16,256]{2,1,0:T(8,128)S(1)} fusion(f32[16,16,256]{2,1,0:T(8,128)S(1)} %fusion.30, f32[16,256,256]{2,1,0:T(8,128)S(1)} %get-tuple-element.6, f32[16,16,256]{2,1,0:T(8,128)S(1)} %gather_fusion.5, f32[16]{0:T(128)S(1)} %copy-done.18), kind=kOutput, calls=%fused_computation.55 | convolution fusion | flops 202506240 | bytes 4980800 | tf_op jit(solution)/shard_map/cpq,rcq->rcp/dot_general | solution.py:66
  143.7 3.5 %fusion.23 = f32[16,2,8,256]{3,2,1,0:T(8,128)S(1)} fusion(f32[16,16,256]{2,1,0:T(8,128)S(1)} %copy-done.8, f32[16,16,256]{2,1,0:T(8,128)S(1)} %fusion.28, f32[16,256,256]{2,1,0:T(8,128)S(1)} %copy-done.3, f32[16,16,256]{2,1,0:T(8,128)S(1)} %copy-done.9, f32[16]{0:T(128)S(1)} %copy-done.21, f32[16,256]{1,0:T(8,128)S(1)} %copy-done.10), kind=kOutput, calls=%fused_computation.50 | convolution fusion | flops 202637312 | bytes 5259328 | tf_op jit(solution)/shard_map/cpq,rcq->rcp/dot_general | solution.py:66
  147.4 21.8 %all-reduce = (f32[16]{0:T(128)S(1)}, f32[16]{0:T(128)S(1)}) all-reduce(f32[16]{0:T(128)S(1)} %get-tuple-element.3, f32[16]{0:T(128)S(1)} %get-tuple-element.2), channel_id=1, replica_groups=mesh['jobs'=2,'clus'=16] {'clus'}, use_global_device_ids=true, to_apply=%region_8.9 | all-reduce | flops 32 | bytes 256 | tf_op jit(solution)/shard_map/psum | solution.py:150
  169.4 24.6 %psum.23 = f32[16]{0:T(128)S(1)} all-reduce(f32[16]{0:T(128)S(1)} %multiply_reduce_fusion.5), channel_id=1, replica_groups=mesh['jobs'=2,'clus'=16] {'clus'}, use_global_device_ids=true, to_apply=%region_12.13 | all-reduce | flops 16 | bytes 128 | tf_op jit(solution)/shard_map/psum | solution.py:155
  194.1 0.8 broadcast_multiply_fusion
  195.5 4.3 %collective-permute-start.10 = (f32[512,16]{0,1:T(8,128)S(1)}, f32[512,16]{0,1:T(8,128)S(1)}, u32[]{:S(2)}, u32[]{:S(2)}) collective-permute-start(f32[512,16]{0,1:T(8,128)S(1)} %reshape.230), channel_id=1, source_target_pairs={{0,4},{1,5},{2,6},{3,7},{4,8},{5,9},{6,10},{7,11},{8,12},{9,13},{1... | collective-permute-start | bytes 98312 | tf_op jit(solution)/shard_map/ppermute | solution.py:18
  199.8 7.1 %collective-permute-start.15 = (f32[512,16]{0,1:T(8,128)S(1)}, f32[512,16]{0,1:T(8,128)S(1)}, u32[]{:S(2)}, u32[]{:S(2)}) collective-permute-start(f32[512,16]{0,1:T(8,128)S(1)} %reshape.230), channel_id=1, source_target_pairs={{4,0},{5,1},{6,2},{7,3},{8,4},{9,5},{10,6},{11,7},{12,8},{13,9},{1... | collective-permute-start | bytes 98312 | tf_op jit(solution)/shard_map/ppermute | solution.py:18
  206.9 7.4 %collective-permute-start.14 = (f32[512,16]{0,1:T(8,128)S(1)}, f32[512,16]{0,1:T(8,128)S(1)}, u32[]{:S(2)}, u32[]{:S(2)}) collective-permute-start(f32[512,16]{0,1:T(8,128)S(1)} %reshape.230), channel_id=1, source_target_pairs={{3,0},{4,1},{5,2},{6,3},{7,4},{8,5},{9,6},{10,7},{11,8},{12,9},{13... | collective-permute-start | bytes 98312 | tf_op jit(solution)/shard_map/ppermute | solution.py:18
  214.4 1.9 collective-permute-start.13
  216.3 4.3 %collective-permute-start.12 = (f32[512,16]{0,1:T(8,128)S(1)}, f32[512,16]{0,1:T(8,128)S(1)}, u32[]{:S(2)}, u32[]{:S(2)}) collective-permute-start(f32[512,16]{0,1:T(8,128)S(1)} %reshape.230), channel_id=1, source_target_pairs={{0,2},{1,3},{2,4},{3,5},{4,6},{5,7},{6,8},{7,9},{8,10},{9,11},{10,... | collective-permute-start | bytes 98312 | tf_op jit(solution)/shard_map/ppermute | solution.py:18
  220.6 1.9 collective-permute-start.11
  222.6 3.2 %collective-permute-done.11 = f32[512,16]{0,1:T(8,128)S(1)} collective-permute-done((f32[512,16]{0,1:T(8,128)S(1)}, f32[512,16]{0,1:T(8,128)S(1)}, u32[]{:S(2)}, u32[]{:S(2)}) %collective-permute-start.11) | collective-permute-done | bytes 32800 | tf_op jit(solution)/shard_map/ppermute | solution.py:18
  225.8 1.9 collective-permute-start.9
  227.8 4.5 %collective-permute-start.8 = (f32[16,4096]{1,0:T(8,128)S(1)}, f32[16,4096]{1,0:T(8,128)S(1)}, u32[]{:S(2)}, u32[]{:S(2)}) collective-permute-start(f32[16,4096]{1,0:T(8,128)S(1)} %get-tuple-element.10), channel_id=1, source_target_pairs={{0,1},{1,2},{2,3},{3,4},{4,5},{5,6},{6,7},{7,8},{8,9},{9,10},{10,1... | collective-permute-start | bytes 786440 | tf_op jit(solution)/shard_map/ppermute | solution.py:29
  232.9 3.1 %gather_fusion.15 = f32[512,16,32]{2,1,0:T(8,128)} fusion(f32[16,32,144]{1,0,2:T(8,128)S(1)} %constant_dynamic-update-slice_fusion.9, s32[1024]{0:T(1024)S(1)} %pad_clamp_fusion), kind=kCustom, calls=%fused_computation.15 | custom fusion | bytes 2099200 | tf_op jit(solution)/shard_map/gather | solution.py:102
  236.0 10.8 %fusion.33 = f32[16,16,32]{2,0,1:T(8,128)S(1)} fusion(f32[16,32,16,32]{1,0,3,2:T(8,128)} %bitcast.146, f32[16,32,32,32]{3,2,1,0:T(8,128)} %multiply_reduce_fusion), kind=kOutput, calls=%fused_computation.60 | convolution fusion | flops 101187584 | bytes 3178496 | tf_op jit(solution)/shard_map/cfab,rbcf->rca/dot_general | solution.py:103
  247.5 0.7 gather_fusion.14
  248.2 0.7 gather_fusion.13
  248.9 0.7 gather_fusion.12
  249.5 0.7 gather_fusion.11
  250.3 5.8 %fusion.4 = f32[16,16,256]{2,1,0:T(8,128)S(1)} fusion(f32[16,256,256]{2,1,0:T(8,128)} %get-tuple-element.7, f32[16,16,256]{2,1,0:T(8,128)S(1)} %gather_fusion.11, f32[16]{0:T(128)S(1)} %copy-done.20), kind=kOutput, calls=%fused_computation.30 | convolution fusion | flops 202440704 | bytes 4718656 | tf_op jit(solution)/shard_map/cpq,rcq->rcp/dot_general | solution.py:66
  256.1 5.8 %fusion.31 = f32[16,16,256]{2,1,0:T(8,128)S(1)} fusion(f32[16,16,256]{2,1,0:T(8,128)S(1)} %fusion.4, f32[16,256,256]{2,1,0:T(8,128)} %copy-done.2, f32[16,16,256]{2,1,0:T(8,128)S(1)} %gather_fusion.12, f32[16]{0:T(128)S(1)} %copy-done.19), kind=kOutput, calls=%fused_computation.58 | convolution fusion | flops 202506240 | bytes 4980800 | tf_op jit(solution)/shard_map/cpq,rcq->rcp/dot_general | solution.py:66
  261.9 3.5 %fusion.29 = f32[16,16,256]{2,1,0:T(8,128)S(1)} fusion(f32[16,16,256]{2,1,0:T(8,128)S(1)} %fusion.31, f32[16,256,256]{2,1,0:T(8,128)S(1)} %copy-done.1, f32[16,16,256]{2,1,0:T(8,128)S(1)} %gather_fusion.13, f32[16]{0:T(128)S(1)} %copy-done.18), kind=kOutput, calls=%fused_computation.56 | convolution fusion | flops 202506240 | bytes 4980800 | tf_op jit(solution)/shard_map/cpq,rcq->rcp/dot_general | solution.py:66
  265.5 3.5 %fusion.27 = f32[16,2,8,256]{3,2,1,0:T(8,128)S(1)} fusion(f32[16,16,256]{2,1,0:T(8,128)S(1)} %fusion.34, f32[16,16,256]{2,1,0:T(8,128)S(1)} %fusion.29, f32[16,256,256]{2,1,0:T(8,128)S(1)} %copy-done.4, f32[16,16,256]{2,1,0:T(8,128)S(1)} %gather_fusion.14, f32[16]{0:T(128)S(1)} %copy-done.21, f32[16,256]{1,0:T(8,128)S(1)} %copy-done.10), kind=kOutput, calls=%fused_computation.54 | convolution fusion | flops 202637312 | bytes 5259328 | tf_op jit(solution)/shard_map/cpq,rcq->rcp/dot_general | solution.py:66
  269.0 0.7 copy.192
  (126 shorter events, 3.9 us)
Async XLA Ops:
  44.0 5.0 %copy-start.7 = (f32[16,4096]{1,0:T(8,128)S(1)}, f32[16,4096]{1,0:T(8,128)}, u32[]{:S(2)}) copy-start(f32[16,4096]{1,0:T(8,128)} %param.11) | copy-start | bytes 786436
  44.0 5.6 %copy-start.6 = (f32[32,4096]{1,0:T(8,128)S(1)}, f32[32,4096]{1,0:T(8,128)}, u32[]{:S(2)}) copy-start(f32[32,4096]{1,0:T(8,128)} %param.10) | copy-start | bytes 1572868
  44.0 20.8 %copy-start.22 = (s32[16,4]{0,1:T(4,128)S(1)}, s32[16,4]{0,1:T(4,128)}, u32[]{:S(2)}) copy-start(s32[16,4]{0,1:T(4,128)} %param.8) | copy-start | bytes 772
  44.0 21.4 %copy-start.13 = (s32[16,32]{1,0:T(8,128)S(1)}, s32[16,32]{1,0:T(8,128)}, u32[]{:S(2)}) copy-start(s32[16,32]{1,0:T(8,128)} %param.9) | copy-start | bytes 6148
  49.0 0.6 copy-start.11
  50.2 29.2 %collective-permute-start.7 = (f32[515,16]{0,1:T(8,128)S(1)}, f32[515,16]{0,1:T(8,128)S(1)}, u32[]{:S(2)}, u32[]{:S(2)}) collective-permute-start(f32[515,16]{0,1:T(8,128)S(1)} %pad_maximum_fusion.4), channel_id=1, source_target_pairs={{4,0},{5,1},{6,2},{7,3},{8,4},{9,5},{10,6},{11,7},{12,8},{13,9},{1... | collective-permute-start | bytes 98888 | tf_op jit(solution)/shard_map/ppermute | solution.py:18
  52.3 27.1 %collective-permute-start.6 = (f32[515,16]{0,1:T(8,128)S(1)}, f32[515,16]{0,1:T(8,128)S(1)}, u32[]{:S(2)}, u32[]{:S(2)}) collective-permute-start(f32[515,16]{0,1:T(8,128)S(1)} %pad_maximum_fusion.4), channel_id=1, source_target_pairs={{3,0},{4,1},{5,2},{6,3},{7,4},{8,5},{9,6},{10,7},{11,8},{12,9},{13... | collective-permute-start | bytes 98888 | tf_op jit(solution)/shard_map/ppermute | solution.py:18
  54.9 24.5 %collective-permute-start.5 = (f32[515,16]{0,1:T(8,128)S(1)}, f32[515,16]{0,1:T(8,128)S(1)}, u32[]{:S(2)}, u32[]{:S(2)}) collective-permute-start(f32[515,16]{0,1:T(8,128)S(1)} %pad_maximum_fusion.4), channel_id=1, source_target_pairs={{2,0},{3,1},{4,2},{5,3},{6,4},{7,5},{8,6},{9,7},{10,8},{11,9},{12,... | collective-permute-start | bytes 98888 | tf_op jit(solution)/shard_map/ppermute | solution.py:18
  57.3 18.1 %collective-permute-start.4 = (f32[515,16]{0,1:T(8,128)S(1)}, f32[515,16]{0,1:T(8,128)S(1)}, u32[]{:S(2)}, u32[]{:S(2)}) collective-permute-start(f32[515,16]{0,1:T(8,128)S(1)} %pad_maximum_fusion.4), channel_id=1, source_target_pairs={{0,2},{1,3},{2,4},{3,5},{4,6},{5,7},{6,8},{7,9},{8,10},{9,11},{10,... | collective-permute-start | bytes 98888 | tf_op jit(solution)/shard_map/ppermute | solution.py:18
  61.3 5.8 %collective-permute-start.2 = (f32[515,16]{0,1:T(8,128)S(1)}, f32[515,16]{0,1:T(8,128)S(1)}, u32[]{:S(2)}, u32[]{:S(2)}) collective-permute-start(f32[515,16]{0,1:T(8,128)S(1)} %pad_maximum_fusion.4), channel_id=1, source_target_pairs={{0,4},{1,5},{2,6},{3,7},{4,8},{5,9},{6,10},{7,11},{8,12},{9,13},{1... | collective-permute-start | bytes 98888 | tf_op jit(solution)/shard_map/ppermute | solution.py:18
  66.4 46.9 %copy-start.15 = (s32[1024]{0:T(1024)}, s32[1024]{0:T(1024)S(1)}, u32[]{:S(2)}) copy-start(s32[1024]{0:T(1024)S(1)} %get-tuple-element.32) | copy-start | bytes 12292
  66.4 48.1 %copy-start.14 = (s32[1024]{0:T(1024)}, s32[1024]{0:T(1024)S(1)}, u32[]{:S(2)}) copy-start(s32[1024]{0:T(1024)S(1)} %get-tuple-element.33) | copy-start | bytes 12292
  66.4 44.4 %copy-start.17 = (s32[1024]{0:T(1024)}, s32[1024]{0:T(1024)S(1)}, u32[]{:S(2)}) copy-start(s32[1024]{0:T(1024)S(1)} %get-tuple-element.30) | copy-start | bytes 12292
  66.4 45.7 %copy-start.16 = (s32[1024]{0:T(1024)}, s32[1024]{0:T(1024)S(1)}, u32[]{:S(2)}) copy-start(s32[1024]{0:T(1024)S(1)} %get-tuple-element.31) | copy-start | bytes 12292
  67.1 5.6 %collective-permute-start.3 = (f32[515,16]{0,1:T(8,128)S(1)}, f32[515,16]{0,1:T(8,128)S(1)}, u32[]{:S(2)}, u32[]{:S(2)}) collective-permute-start(f32[515,16]{0,1:T(8,128)S(1)} %pad_maximum_fusion.4), channel_id=1, source_target_pairs={{0,3},{1,4},{2,5},{3,6},{4,7},{5,8},{6,9},{7,10},{8,11},{9,12},{10... | collective-permute-start | bytes 98888 | tf_op jit(solution)/shard_map/ppermute | solution.py:18
  72.7 34.8 %collective-permute-start.1 = (f32[19,4096]{1,0:T(8,128)}, f32[19,4096]{1,0:T(8,128)S(1)}, u32[]{:S(2)}, u32[]{:S(2)}) collective-permute-start(f32[19,4096]{1,0:T(8,128)} %pad_maximum_fusion.2), channel_id=1, source_target_pairs={{1,0},{2,1},{3,2},{4,3},{5,4},{6,5},{7,6},{8,7},{9,8},{10,9},{11,1... | collective-permute-start | bytes 933896 | tf_op jit(solution)/shard_map/ppermute | solution.py:31
  75.4 32.1 %collective-permute-start = (f32[19,4096]{1,0:T(8,128)}, f32[19,4096]{1,0:T(8,128)}, u32[]{:S(2)}, u32[]{:S(2)}) collective-permute-start(f32[19,4096]{1,0:T(8,128)} %pad_maximum_fusion.2), channel_id=1, source_target_pairs={{0,1},{1,2},{2,3},{3,4},{4,5},{5,6},{6,7},{7,8},{8,9},{9,10},{10,1... | collective-permute-start | bytes 933896 | tf_op jit(solution)/shard_map/ppermute | solution.py:29
  85.9 9.7 %copy-start.5 = (f32[512,16,32]{2,1,0:T(8,128)S(1)}, f32[512,16,32]{2,1,0:T(8,128)}, u32[]{:S(2)}) copy-start(f32[512,16,32]{2,1,0:T(8,128)} %gather_fusion.9) | copy-start | bytes 3145732
  127.9 12.3 %copy-start.2 = (f32[16,256,256]{2,1,0:T(8,128)}, f32[16,256,256]{2,1,0:T(8,128)S(1)}, u32[]{:S(2)}) copy-start(f32[16,256,256]{2,1,0:T(8,128)S(1)} %get-tuple-element.5) | copy-start | bytes 12582916
  127.9 12.3 %copy-start = (f32[16,256,256]{2,1,0:T(8,128)}, f32[16,256,256]{2,1,0:T(8,128)S(1)}, u32[]{:S(2)}) copy-start(f32[16,256,256]{2,1,0:T(8,128)S(1)} %get-tuple-element.6) | copy-start | bytes 12582916
  127.9 8.7 %copy-start.19 = (f32[16]{0:T(128)S(1)}, f32[16]{0:T(128)}, u32[]{:S(2)}) copy-start(f32[16]{0:T(128)} %get-tuple-element.24) | copy-start | bytes 196
  127.9 12.3 %copy-start.18 = (f32[16]{0:T(128)S(1)}, f32[16]{0:T(128)}, u32[]{:S(2)}) copy-start(f32[16]{0:T(128)} %get-tuple-element.25) | copy-start | bytes 196
  136.6 7.1 %copy-start.3 = (f32[16,256,256]{2,1,0:T(8,128)S(1)}, f32[16,256,256]{2,1,0:T(8,128)}, u32[]{:S(2)}) copy-start(f32[16,256,256]{2,1,0:T(8,128)} %get-tuple-element.4) | copy-start | bytes 12582916
  136.6 7.1 %copy-start.8 = (f32[16,16,256]{2,1,0:T(8,128)S(1)}, f32[16,16,256]{2,1,0:T(8,128)}, u32[]{:S(2)}) copy-start(f32[16,16,256]{2,1,0:T(8,128)} %fusion.37) | copy-start | bytes 786436
  136.6 7.1 %copy-start.9 = (f32[16,16,256]{2,1,0:T(8,128)S(1)}, f32[16,16,256]{2,1,0:T(8,128)}, u32[]{:S(2)}) copy-start(f32[16,16,256]{2,1,0:T(8,128)} %gather_fusion.7) | copy-start | bytes 786436
  136.6 7.1 %copy-start.10 = (f32[16,256]{1,0:T(8,128)S(1)}, f32[16,256]{1,0:T(8,128)}, u32[]{:S(2)}) copy-start(f32[16,256]{1,0:T(8,128)} %sqrt.62) | copy-start | bytes 49156
  136.6 7.1 %copy-start.21 = (f32[16]{0:T(128)S(1)}, f32[16]{0:T(128)}, u32[]{:S(2)}) copy-start(f32[16]{0:T(128)} %get-tuple-element.22) | copy-start | bytes 196
  143.7 50.4 %copy-start.12 = (f32[4096]{0:T(1024)S(1)}, f32[4096]{0:T(1024)}, u32[]{:S(2)}) copy-start(f32[4096]{0:T(1024)} %copy-done.11) | copy-start | bytes 49156
  195.5 25.0 %collective-permute-start.10 = (f32[512,16]{0,1:T(8,128)S(1)}, f32[512,16]{0,1:T(8,128)S(1)}, u32[]{:S(2)}, u32[]{:S(2)}) collective-permute-start(f32[512,16]{0,1:T(8,128)S(1)} %reshape.230), channel_id=1, source_target_pairs={{0,4},{1,5},{2,6},{3,7},{4,8},{5,9},{6,10},{7,11},{8,12},{9,13},{1... | collective-permute-start | bytes 98312 | tf_op jit(solution)/shard_map/ppermute | solution.py:18
  199.8 33.0 %collective-permute-start.15 = (f32[512,16]{0,1:T(8,128)S(1)}, f32[512,16]{0,1:T(8,128)S(1)}, u32[]{:S(2)}, u32[]{:S(2)}) collective-permute-start(f32[512,16]{0,1:T(8,128)S(1)} %reshape.230), channel_id=1, source_target_pairs={{4,0},{5,1},{6,2},{7,3},{8,4},{9,5},{10,6},{11,7},{12,8},{13,9},{1... | collective-permute-start | bytes 98312 | tf_op jit(solution)/shard_map/ppermute | solution.py:18
  206.9 25.7 %collective-permute-start.14 = (f32[512,16]{0,1:T(8,128)S(1)}, f32[512,16]{0,1:T(8,128)S(1)}, u32[]{:S(2)}, u32[]{:S(2)}) collective-permute-start(f32[512,16]{0,1:T(8,128)S(1)} %reshape.230), channel_id=1, source_target_pairs={{3,0},{4,1},{5,2},{6,3},{7,4},{8,5},{9,6},{10,7},{11,8},{12,9},{13... | collective-permute-start | bytes 98312 | tf_op jit(solution)/shard_map/ppermute | solution.py:18
  214.4 18.2 %collective-permute-start.13 = (f32[512,16]{0,1:T(8,128)S(1)}, f32[512,16]{0,1:T(8,128)S(1)}, u32[]{:S(2)}, u32[]{:S(2)}) collective-permute-start(f32[512,16]{0,1:T(8,128)S(1)} %reshape.230), channel_id=1, source_target_pairs={{2,0},{3,1},{4,2},{5,3},{6,4},{7,5},{8,6},{9,7},{10,8},{11,9},{12,... | collective-permute-start | bytes 98312 | tf_op jit(solution)/shard_map/ppermute | solution.py:18
  216.3 11.5 %collective-permute-start.12 = (f32[512,16]{0,1:T(8,128)S(1)}, f32[512,16]{0,1:T(8,128)S(1)}, u32[]{:S(2)}, u32[]{:S(2)}) collective-permute-start(f32[512,16]{0,1:T(8,128)S(1)} %reshape.230), channel_id=1, source_target_pairs={{0,2},{1,3},{2,4},{3,5},{4,6},{5,7},{6,8},{7,9},{8,10},{9,11},{10,... | collective-permute-start | bytes 98312 | tf_op jit(solution)/shard_map/ppermute | solution.py:18
  220.6 5.2 %collective-permute-start.11 = (f32[512,16]{0,1:T(8,128)S(1)}, f32[512,16]{0,1:T(8,128)S(1)}, u32[]{:S(2)}, u32[]{:S(2)}) collective-permute-start(f32[512,16]{0,1:T(8,128)S(1)} %reshape.230), channel_id=1, source_target_pairs={{0,3},{1,4},{2,5},{3,6},{4,7},{5,8},{6,9},{7,10},{8,11},{9,12},{10... | collective-permute-start | bytes 98312 | tf_op jit(solution)/shard_map/ppermute | solution.py:18
  225.8 21.5 %collective-permute-start.9 = (f32[16,4096]{1,0:T(8,128)S(1)}, f32[16,4096]{1,0:T(8,128)S(1)}, u32[]{:S(2)}, u32[]{:S(2)}) collective-permute-start(f32[16,4096]{1,0:T(8,128)S(1)} %get-tuple-element.10), channel_id=1, source_target_pairs={{1,0},{2,1},{3,2},{4,3},{5,4},{6,5},{7,6},{8,7},{9,8},{10,9},{11,1... | collective-permute-start | bytes 786440 | tf_op jit(solution)/shard_map/ppermute | solution.py:31
  227.8 19.4 %collective-permute-start.8 = (f32[16,4096]{1,0:T(8,128)S(1)}, f32[16,4096]{1,0:T(8,128)S(1)}, u32[]{:S(2)}, u32[]{:S(2)}) collective-permute-start(f32[16,4096]{1,0:T(8,128)S(1)} %get-tuple-element.10), channel_id=1, source_target_pairs={{0,1},{1,2},{2,3},{3,4},{4,5},{5,6},{6,7},{7,8},{8,9},{9,10},{10,1... | collective-permute-start | bytes 786440 | tf_op jit(solution)/shard_map/ppermute | solution.py:29
  246.9 3.4 %copy-start.20 = (f32[16]{0:T(128)S(1)}, f32[16]{0:T(128)}, u32[]{:S(2)}) copy-start(f32[16]{0:T(128)} %get-tuple-element.23) | copy-start | bytes 196
  250.3 11.7 %copy-start.1 = (f32[16,256,256]{2,1,0:T(8,128)S(1)}, f32[16,256,256]{2,1,0:T(8,128)}, u32[]{:S(2)}) copy-start(f32[16,256,256]{2,1,0:T(8,128)} %copy-done) | copy-start | bytes 12582916
  256.1 9.4 %copy-start.4 = (f32[16,256,256]{2,1,0:T(8,128)S(1)}, f32[16,256,256]{2,1,0:T(8,128)}, u32[]{:S(2)}) copy-start(f32[16,256,256]{2,1,0:T(8,128)} %get-tuple-element.4) | copy-start | bytes 12582916
where the time goes:
time: 273 us; the launch traced here: 270 us
  local copies, waits for them, and re-layouts  68 us (25%)
  matrix products  62 us (23%)
  starting transfers between devices  58.3 us (21%)
  blocking collectives  46.4 us (17%)
  other arithmetic  28.5 us (10%)
  waiting for transfers between devices  4.92 us (2%)
    gather x2, local copies, waits for them, and re-layouts, geometry(): corners = vertices[:, corner_index]  45.8 us
    ppermute x12, starting transfers between devices, from_behind(): lax.ppermute(value, axis, [(source, source + steps) for source in range(f...  45.2 us
    dot_general x8, matrix products, near_term(): jnp.einsum('cpq,rcq->rcp', kernel, masked, precision=HIGHEST_PRECISION)  37.8 us
    psum x1, blocking collectives, body(): energy = lax.psum(jnp.sum(residual * residual, axis=1), 'clus')  24.6 us
    psum x1, blocking collectives, body(): lax.psum((jnp.sum(krylov * image, axis=1), jnp.sum(krylov * krylov, axis=...  21.8 us
    dot_general x2, matrix products, far_part(): jnp.einsum('cfab,rbcf->rca', coupler, selected, precision=HIGHEST_PRECISION)  21.5 us
    reduce_sum x1, other arithmetic, near_term(): kernel = 1.0 / jnp.sqrt(jnp.sum(offsets * offsets, axis=0) + SMOOTHING)  11.4 us
    reduce_sum x1, other arithmetic, coupling(): return 1.0 / jnp.sqrt(jnp.sum(offsets * offsets, axis=0) + SMOOTHING)  9.72 us
  transfers between devices with their start and end apart: 16, of which 2 were waited for; matrix products, arithmetic and copies ran while one was open for 17% of the time, Pallas kernels for 0%

commit v1 on v0

v1 whole, which is shorter than its diff:
```python
import functools

import jax
import jax.numpy as jnp
import numpy as np
from jax import lax
from jax.experimental import pallas as pl
from jax.experimental.pallas import tpu as pltpu
from jax.sharding import PartitionSpec as P

REACH = 4
SMOOTHING = 0.04
COULOMB = 2.0
PROXY_RADIUS = 0.6
LANES = 128
F32 = jnp.float32
BF16 = jnp.bfloat16


def proxy_offsets(points):
    counter = np.arange(points, dtype=np.float32)
    height = 1.0 - (2.0 * counter + 1.0) / points
    radial = np.sqrt(1.0 - height * height)
    azimuth = counter * 2.399963
    return PROXY_RADIUS * np.stack([radial * np.cos(azimuth), radial * np.sin(azimuth), height]).astype(np.float32)


def split(value):
    high = value.astype(BF16)
    return high, (value - high.astype(F32)).astype(BF16)


def stacked(value):
    return jnp.concatenate(split(value), axis=0)


def folded(value):
    half = value.shape[0] // 2
    return value[:half] + value[half:]


def dot_nt(left, right):
    return lax.dot_general(left, right, (((1,), (1,)), ((), ())), preferred_element_type=F32)


def dot_nn(left, right):
    return lax.dot_general(left, right, (((1,), (0,)), ((), ())), preferred_element_type=F32)


def moments_of(weighted, basis_block):
    pieces = stacked(weighted)
    high, low = split(basis_block)
    return folded(dot_nt(pieces, high) + dot_nt(pieces, low))


def prepare_kernel(cl, vcl, rank, base_ref, vertices_ref, corners_ref, krylov_ref, basis_ref, charges_ref, centroid_ref, table_ref, area_ref):
    clusters = krylov_ref.shape[1] // cl
    rhs = krylov_ref.shape[0]
    base = base_ref[0]
    table_ref[rhs:, :] = jnp.zeros_like(table_ref[rhs:, :])
    for c in range(clusters):
        mesh = vertices_ref[:, c * vcl:(c + 1) * vcl]
        tables = [jnp.broadcast_to(mesh[k:k + 1, :], (8, vcl)) for k in range(3)]
        sums = [jnp.zeros((1, 1), F32)] * 3
        for h in range(cl // LANES):
            lanes = slice(c * cl + h * LANES, c * cl + (h + 1) * LANES)
            local = corners_ref[:, lanes] - (base + c * vcl)
            local = jnp.concatenate([local, local, local[:2]], axis=0)
            first, edge_one, edge_two = [], [], []
            for k in range(3):
                corner = jnp.take_along_axis(tables[k], local, axis=1, mode="promise_in_bounds")
                middle = (corner[0:1] + corner[1:2] + corner[2:3]) / 3.0
                centroid_ref[c:c + 1, k * cl + h * LANES:k * cl + (h + 1) * LANES] = middle
                sums[k] = sums[k] + jnp.sum(middle, axis=1, keepdims=True)
                edge_one.append(corner[1:2] - corner[0:1])
                edge_two.append(corner[2:3] - corner[0:1])
            normal = [
                edge_one[1] * edge_two[2] - edge_one[2] * edge_two[1],
                edge_one[2] * edge_two[0] - edge_one[0] * edge_two[2],
                edge_one[0] * edge_two[1] - edge_one[1] * edge_two[0],
            ]
            area = 0.5 * jnp.sqrt(normal[0] * normal[0] + normal[1] * normal[1] + normal[2] * normal[2])
            area_ref[:, lanes] = jnp.broadcast_to(area, (8, LANES))
            charges_ref[:, lanes] = area * krylov_ref[:, lanes]
        for k in range(3):
            table_ref[rhs + k:rhs + k + 1, c * rank:(c + 1) * rank] = jnp.broadcast_to(sums[k] / cl, (1, rank))
        panels = slice(c * cl, (c + 1) * cl)
        table_ref[0:rhs, c * rank:(c + 1) * rank] = moments_of(charges_ref[:, panels], basis_ref[:, panels])


def columns_of(centroid_ref, row, cl, columns_ref, at):
    rows = jnp.concatenate([centroid_ref[row:row + 1, k * cl:(k + 1) * cl] for k in range(3)] * 2 + [centroid_ref[row:row + 1, 0:cl]] * 2, axis=0)
    upright = jnp.transpose(rows)
    for k in range(3):
        columns_ref[at, k] = jnp.broadcast_to(upright[:, k:k + 1], (cl, LANES))


def near_block(columns, source, cl, out_ref, at):
    for h in range(cl // LANES):
        lanes = slice(h * LANES, (h + 1) * LANES)
        gap = [columns[k] - source(k, h) for k in range(3)]
        square = gap[0] * gap[0] + gap[1] * gap[1] + gap[2] * gap[2]
        high, low = split(lax.rsqrt(square + SMOOTHING))
        out_ref[at, 0:cl, lanes] = high
        out_ref[at, cl:2 * cl, lanes] = low


def near_product(pieces, block_ref, at, cl):
    return dot_nt(pieces, block_ref[at, 0:cl, :]) + dot_nt(pieces, block_ref[at, cl:2 * cl, :])


def self_kernel(cl, charges_ref, centroid_ref, blocks_ref, near_ref, columns_ref):
    clusters = charges_ref.shape[1] // cl
    for c in range(clusters):
        columns_of(centroid_ref, c, cl, columns_ref, c % 2)
        source = lambda k, h: centroid_ref[c:c + 1, k * cl + h * LANES:k * cl + (h + 1) * LANES]
        near_block([columns_ref[c % 2, k] for k in range(3)], source, cl, blocks_ref, c)
        panels = slice(c * cl, (c + 1) * cl)
        near_ref[:, panels] = folded(near_product(stacked(charges_ref[:, panels]), blocks_ref, c, cl))


def fill_charges(pieces_ref, blocks, clusters, cl):
    for b, ref in enumerate(blocks):
        for c in range(clusters):
            pieces_ref[b * clusters + c] = stacked(ref[:, c * cl:(c + 1) * cl])
    pieces_ref[3 * clusters] = jnp.zeros_like(pieces_ref[3 * clusters])


def list_pairs(near_ref, base, clusters, list_ref):
    slots = near_ref.shape[1]

    def put(n, c, j):
        list_ref[0, n] = c
        list_ref[1, n] = j

    def step(i, n):
        c = i // (slots - 1)
        j = near_ref[c, 1 + i % (slots - 1)]
        put(n, c, j - base)
        return n + (j >= 0).astype(jnp.int32)

    count = lax.fori_loop(0, clusters * (slots - 1), step, jnp.int32(0))
    put(count, 0, 3 * clusters)
    return count


def remote_kernel(cl, base_ref, near_ref, own_ref, left_ref, right_ref, own_centroid_ref, left_centroid_ref, right_centroid_ref, start_ref,
                  blocks_ref, near_out_ref, pieces_ref, sources_ref, columns_ref, even_ref, odd_ref, total_ref, list_ref, sems):
    clusters = own_ref.shape[1] // cl
    rhs = own_ref.shape[0]
    count = list_pairs(near_ref, base_ref[0], clusters, list_ref)
    for b, ref in enumerate((left_centroid_ref, own_centroid_ref, right_centroid_ref)):
        for c in range(clusters):
            for k in range(3):
                sources_ref[b * clusters + c, k:k + 1, :] = ref[c:c + 1, k * cl:(k + 1) * cl]
    sources_ref[3 * clusters] = jnp.zeros_like(sources_ref[3 * clusters])
    fill_charges(pieces_ref, (left_ref, own_ref, right_ref), clusters, cl)
    for c in range(clusters):
        columns_of(own_centroid_ref, c, cl, columns_ref, c)
        total_ref[c] = jnp.zeros_like(total_ref[c])
    steps = (count + 1) // 2

    def build(ref, m, which):
        c, j = list_ref[0, 2 * m + which], list_ref[1, 2 * m + which]
        source = lambda k, h: sources_ref[j, k:k + 1, h * LANES:(h + 1) * LANES]
        near_block([columns_ref[c, k] for k in range(3)], source, cl, ref, m)

    def apply(ref, m, which):
        c, j = list_ref[0, 2 * m + which], list_ref[1, 2 * m + which]
        total_ref[c] += near_product(pieces_ref[j], ref, m, cl)

    def send(ref, m, which):
        return pltpu.make_async_copy(ref.at[m], blocks_ref.at[2 * m + which], sems.at[which])

    def step(m, _):
        build(even_ref, m, 0)
        send(even_ref, m, 0).start()
        apply(even_ref, m, 0)
        build(odd_ref, m, 1)
        send(odd_ref, m, 1).start()
        apply(odd_ref, m, 1)
        return 0

    lax.fori_loop(0, steps, step, 0)
    for c in range(clusters):
        panels = slice(c * cl, (c + 1) * cl)
        near_out_ref[:, panels] = start_ref[:, panels] + folded(total_ref[c])

    def drain(m, _):
        send(even_ref, m, 0).wait()
        send(odd_ref, m, 1).wait()
        return 0

    lax.fori_loop(0, steps, drain, 0)


def gather_tables(position, far_ref, table_ref, rank, pieces_ref, middle_ref, each):
    devices, _, span = table_ref.shape
    rhs = pieces_ref.shape[1] // 2
    per = LANES // rank
    groups = span // LANES
    clusters = far_ref.shape[0]
    window = 2 * REACH + 1

    def load(b, _):
        block = jnp.clip(position - REACH + b, 0, devices - 1)
        for g in range(groups):
            tile = table_ref[block, :, g * LANES:(g + 1) * LANES]
            for s in range(per):
                turned = pltpu.roll(tile, s * rank, 1) if s else tile
                at = (s * window + b) * groups + g
                pieces_ref[at] = stacked(turned[:rhs])
                if middle_ref is not None:
                    middle_ref[at] = turned[rhs:]
        return 0

    lax.fori_loop(0, window, load, 0)
    lane = lax.broadcasted_iota(jnp.int32, (1, LANES), 1) // rank
    base = (position - REACH) * clusters

    def cluster(c, _):
        rows, centers = [], []
        for g in range(far_ref.shape[1] // per):
            row = center = None
            for u in range(per):
                j = far_ref[c, g * per + u] - base
                at = lax.rem(u - j + 4 * per * window * clusters, per) * (window * groups) + j // per
                take = pieces_ref[at]
                row = take if row is None else jnp.where(lane == u, take, row)
                if middle_ref is not None:
                    take = middle_ref[at]
                    center = take if center is None else jnp.where(lane == u, take, center)
            rows.append(row)
            centers.append(center)
        each(c, jnp.concatenate(rows, axis=1), centers)
        return 0

    lax.fori_loop(0, clusters, cluster, 0)


def far_potential(gathered, coupling, basis_block, rank):
    field = folded(dot_nt(gathered, coupling))
    field = stacked(field[:, 0:rank] + field[:, rank:2 * rank])
    high, low = split(basis_block)
    return folded(dot_nn(field, high) + dot_nn(field, low))


def image_kernel(cl, rank, position_ref, far_ref, table_ref, own_table_ref, basis_ref, area_ref, near_ref, krylov_ref, upright_ref, flat_ref,
                 image_ref, charges_ref, moments_ref, coupling_ref, pieces_ref, middle_ref):
    rhs = krylov_ref.shape[0]
    clusters = krylov_ref.shape[1] // cl
    span = clusters * rank

    def each(c, gathered, centers):
        panels = pl.ds(pl.multiple_of(c * cl, cl), cl)
        mine = [jnp.broadcast_to(own_table_ref[c, k:k + 1, :], (1, LANES)) for k in range(3)]
        for g, center in enumerate(centers):
            square = SMOOTHING
            for k in range(3):
                gap = (center[k:k + 1] - mine[k] + flat_ref[k:k + 1, :]) - upright_ref[k]
                square = square + gap * gap
            high, low = split(lax.rsqrt(square))
            coupling_ref[c, 0:rank, g * LANES:(g + 1) * LANES] = high
            coupling_ref[c, rank:2 * rank, g * LANES:(g + 1) * LANES] = low
        far = far_potential(gathered, coupling_ref[c], basis_ref[:, panels], rank)
        area = area_ref[0:1, panels]
        image = COULOMB * area * (near_ref[:, panels] + far)
        image_ref[:, panels] = image
        charges_ref[:, panels] = area * image

    gather_tables(position_ref[0], far_ref, table_ref, rank, pieces_ref, middle_ref, each)
    for c in range(clusters):
        panels = slice(c * cl, (c + 1) * cl)
        moments_ref[:, c * rank:(c + 1) * rank] = moments_of(charges_ref[:, panels], basis_ref[:, panels])
    image, krylov = image_ref[...], krylov_ref[...]
    squared = jnp.sum(krylov * krylov, axis=1, keepdims=True)
    correlation = jnp.sum(krylov * image, axis=1, keepdims=True)
    local = jnp.where(squared > 0, correlation / jnp.where(squared > 0, squared, 1.0), 0.0)
    residual = image - local * krylov
    energy = jnp.sum(residual * residual, axis=1, keepdims=True)
    lane = lax.broadcasted_iota(jnp.int32, (rhs, LANES), 1)
    moments_ref[:, span:] = jnp.where(lane == 0, squared, jnp.where(lane == 1, local, jnp.where(lane == 2, energy, correlation)))


def self_again_kernel(cl, charges_ref, blocks_ref, near_ref):
    clusters = charges_ref.shape[1] // cl
    for c in range(clusters):
        panels = slice(c * cl, (c + 1) * cl)
        near_ref[:, panels] = folded(near_product(stacked(charges_ref[:, panels]), blocks_ref, c, cl))


def finish_kernel(cl, rank, position_ref, base_ref, near_ref, far_ref, blocks_ref, own_ref, left_ref, right_ref, start_ref, table_ref, coupling_ref,
                  basis_ref, area_ref, image_ref, krylov_ref, next_ref, second_ref, held_ref, charge_ref, pieces_ref, total_ref, list_ref, sems):
    rhs = krylov_ref.shape[0]
    clusters = krylov_ref.shape[1] // cl
    span = clusters * rank
    devices = table_ref.shape[0]
    count = list_pairs(near_ref, base_ref[0], clusters, list_ref)
    steps = (count + 1) // 2

    def fetch(i):
        return pltpu.make_async_copy(blocks_ref.at[i], held_ref.at[i], sems.at[i])

    def begin(m, _):
        fetch(2 * m).start()
        fetch(2 * m + 1).start()
        return 0

    lax.fori_loop(0, steps, begin, 0)

    def add(d, sums):
        return sums[0] + table_ref[d, :, span:], sums[1]

    squared = correlation = jnp.zeros((rhs, 1), F32)
    for d in range(devices):
        squared = squared + table_ref[d, :, span:span + 1]
        correlation = correlation + table_ref[d, :, span + 3:span + 4]
    projection = correlation / (squared + 1e-06)
    energy = jnp.zeros((rhs, 1), F32)
    for d in range(devices):
        gap = projection - table_ref[d, :, span + 1:span + 2]
        energy = energy + table_ref[d, :, span + 2:span + 3] + gap * gap * table_ref[d, :, span:span + 1]
    scaling = jnp.sqrt(energy / (krylov_ref.shape[1] * devices) + 1e-06)
    next_ref[...] = (image_ref[...] - projection * krylov_ref[...]) / scaling
    fill_charges(charge_ref, (left_ref, own_ref, right_ref), clusters, cl)
    for c in range(clusters):
        total_ref[c] = jnp.zeros_like(total_ref[c])

    def step(m, _):
        for which in range(2):
            i = 2 * m + which
            fetch(i).wait()
            c, j = list_ref[0, i], list_ref[1, i]
            total_ref[c] += near_product(charge_ref[j], held_ref, i, cl)
        return 0

    lax.fori_loop(0, steps, step, 0)

    def each(c, gathered, _):
        panels = pl.ds(pl.multiple_of(c * cl, cl), cl)
        far = far_potential(gathered, coupling_ref[c], basis_ref[:, panels], rank)
        image = COULOMB * area_ref[0:1, panels] * (start_ref[:, panels] + folded(total_ref[c]) + far)
        second_ref[:, panels] = (image - projection * image_ref[:, panels]) / scaling

    gather_tables(position_ref[0], far_ref, table_ref.at[:, :, 0:span], rank, pieces_ref, None, each)


def call(kernel, outs, scratch, memory, *args, limit=48):
    spaces = {"s": pltpu.SMEM, "v": pltpu.VMEM, "a": pl.ANY}
    ins, out_spaces = memory.split(">")
    return pl.pallas_call(
        kernel,
        out_shape=[jax.ShapeDtypeStruct(*out) for out in outs],
        in_specs=[pl.BlockSpec(memory_space=spaces[m]) for m in ins],
        out_specs=[pl.BlockSpec(memory_space=spaces[m]) for m in out_spaces],
        scratch_shapes=scratch,
        compiler_params=pltpu.CompilerParams(vmem_limit_bytes=limit * 2 ** 20),
    )(*args)


def body(vertices, panel_vertices, near_pairs, far_pairs, basis, krylov):
    clusters, slots = near_pairs.shape
    partners = far_pairs.shape[1]
    rhs, panels = krylov.shape
    rank = basis.shape[0]
    cl = panels // clusters
    vcl = vertices.shape[1] // clusters
    span = clusters * rank
    devices = lax.axis_size("clus")
    position = lax.axis_index("clus")
    place = position.reshape(1).astype(jnp.int32)
    base = ((position - 1) * clusters).reshape(1).astype(jnp.int32)
    corner_base = (position * vertices.shape[1]).reshape(1).astype(jnp.int32)
    offsets = proxy_offsets(rank)
    upright = jnp.asarray(np.ascontiguousarray(np.broadcast_to(offsets[:, :, None], (3, rank, LANES))))
    flat = jnp.asarray(np.concatenate([np.tile(offsets, (1, LANES // rank)), np.zeros((5, LANES), np.float32)]))
    live = clusters * (slots - 1) + 2
    window = (2 * REACH + 1) * (LANES // rank) * (span // LANES)
    bf_block = (2 * cl, cl)

    charges, centroid, table, area = call(
        functools.partial(prepare_kernel, cl, vcl, rank),
        [((rhs, panels), F32), ((clusters, 3 * cl), F32), ((rhs + 8, span), F32), ((8, panels), F32)],
        [],
        "svvvv>vvvv",
        corner_base, vertices, panel_vertices, krylov, basis,
    )

    def shifted(value, steps):
        return lax.ppermute(value, "clus", [(i, i + steps) for i in range(devices) if 0 <= i + steps < devices])

    packed = jnp.concatenate([charges, centroid], axis=1)
    left, right = shifted(packed, 1), shifted(packed, -1)
    tables = lax.all_gather(table, "clus", axis=0)
    own_blocks, near = call(
        functools.partial(self_kernel, cl),
        [((clusters,) + bf_block, BF16), ((rhs, panels), F32)],
        [pltpu.VMEM((2, 3, cl, LANES), F32)],
        "vv>vv",
        charges, centroid,
    )
    blocks, near = call(
        functools.partial(remote_kernel, cl),
        [((live,) + bf_block, BF16), ((rhs, panels), F32)],
        [
            pltpu.VMEM((3 * clusters + 1, 2 * rhs, cl), BF16),
            pltpu.VMEM((3 * clusters + 1, 8, cl), F32),
            pltpu.VMEM((clusters, 3, cl, LANES), F32),
            pltpu.VMEM((live // 2,) + bf_block, BF16),
            pltpu.VMEM((live // 2,) + bf_block, BF16),
            pltpu.VMEM((clusters, 2 * rhs, cl), F32),
            pltpu.SMEM((2, live), jnp.int32),
            pltpu.SemaphoreType.DMA((2,)),
        ],
        "ssvvvvvvv>av",
        base, near_pairs, charges, left[:, :panels], right[:, :panels], centroid, left[:, panels:], right[:, panels:], near,
    )
    centers = jnp.transpose(table[rhs:].reshape(8, clusters, rank), (1, 0, 2))[:, :, 0:1]
    image, second_charges, moments, coupling = call(
        functools.partial(image_kernel, cl, rank),
        [((rhs, panels), F32), ((rhs, panels), F32), ((rhs, span + LANES), F32), ((clusters, 2 * rank, partners * rank), BF16)],
        [pltpu.VMEM((window, 2 * rhs, LANES), BF16), pltpu.VMEM((window, 8, LANES), F32)],
        "ssvvvvvvvv>vvvv",
        place, far_pairs, tables, centers, basis, area, near, krylov, upright, flat,
    )
    left, right = shifted(second_charges, 1), shifted(second_charges, -1)
    tables = lax.all_gather(moments, "clus", axis=0)
    (near,) = call(
        functools.partial(self_again_kernel, cl),
        [((rhs, panels), F32)],
        [],
        "vv>v",
        second_charges, own_blocks,
    )
    return tuple(call(
        functools.partial(finish_kernel, cl, rank),
        [((rhs, panels), F32), ((rhs, panels), F32)],
        [
            pltpu.VMEM((live,) + bf_block, BF16),
            pltpu.VMEM((3 * clusters + 1, 2 * rhs, cl), BF16),
            pltpu.VMEM((window, 2 * rhs, LANES), BF16),
            pltpu.VMEM((clusters, 2 * rhs, cl), F32),
            pltpu.SMEM((2, live), jnp.int32),
            pltpu.SemaphoreType.DMA((live,)),
        ],
        "ssssavvvvvvvvvv>vv",
        place, base, near_pairs, far_pairs, blocks, second_charges, left, right, near, tables, coupling, basis, area, image, krylov,
    ))


def solution(mesh):
    whole = P(None, ("jobs", "clus"))
    rows = P(("jobs", "clus"), None)
    return jax.shard_map(
        body,
        mesh=mesh,
        in_specs=(whole, whole, rows, rows, whole, whole),
        out_specs=(whole, whole),
        check_vma=False,
    )
```

time: 273 us -> 118 us (0.43)
  the two profiles are of different devices: /device:TPU:13 before, /device:TPU:3 now
where the time goes in v1:
time: 118 us; the launch traced here: 119 us
  Pallas kernels  58 us (49%)
  blocking collectives  42.4 us (36%)
  starting transfers between devices  11.2 us (9%)
  local copies, waits for them, and re-layouts  6.51 us (6%)
    pallas_call x6, Pallas kernels, call(): pl.pallas_call(kernel, out_shape=[jax.ShapeDtypeStruct(*out) for out in o...  58 us
    all_gather x1, blocking collectives, body(): tables = lax.all_gather(table, 'clus', axis=0)  23.2 us
    all_gather x1, blocking collectives, body(): tables = lax.all_gather(moments, 'clus', axis=0)  19.2 us
    ppermute x4, starting transfers between devices, shifted(): lax.ppermute(value, 'clus', [(i, i + steps) for i in range(devices) if 0...  11.2 us
    unnamed x24, local copies, waits for them, and re-layouts  6.35 us
  transfers between devices with their start and end apart: 4, of which 0 were waited for; matrix products, arithmetic and copies ran while one was open for 1% of the time, Pallas kernels for 4%

profile of v1, /device:TPU:3, one launch (start us, length us, event | category | flops | bytes accessed | tf_op | source)
XLA Modules:
  0.0 119.0 jit_solution(15691321441827848919)
XLA Ops:
  0.6 0.0 copy-start.8
  0.6 0.0 copy-start
  0.7 1.0 copy-done
  1.7 0.0 copy-start.4
  1.7 0.9 copy-done.4
  2.6 0.0 copy-start.6
  2.6 0.8 copy-done.6
  3.5 0.0 copy-start.9
  3.5 0.8 copy-done.9
  4.2 0.0 copy-start.1
  4.2 0.0 copy-start.5
  4.2 0.0 copy-start.7
  4.2 0.0 copy-start.10
  4.2 5.0 %shard_map.95 = (f32[16,4096]{1,0:T(8,128)S(1)}, f32[16,768]{1,0:T(8,128)S(1)}, f32[24,512]{1,0:T(8,128)S(1)}, f32[8,4096]{1,0:T(8,128)S(1)}) custom-call(s32[1]{0:T(128)} %bitcast.2.base_ref, f32[3,2048]{1,0:T(4,128)S(1)} %copy-done.9, s32[3,4096]{1,0:T(4,128)S(1)} %copy-done.6, f32[16,4096]{1,0:T(8,128)S(1)} %copy-done.4, f32[32,4096]{1,0:T(8,128)S(1)} %copy-done), custom_call_target="tpu_custom_call" | custom-call | tf_op jit(solution)/shard_map/pallas_call | solution.py:351
  9.3 2.6 %collective-permute-start.1 = (f32[16,4864]{1,0:T(8,128)S(1)}, f32[16,4864]{1,0:T(8,128)S(1)}, u32[]{:S(2)}, u32[]{:S(2)}) collective-permute-start(f32[16,4864]{1,0:T(8,128)S(1)} %constant_dynamic-update-slice_fusion), channel_id=1, source_target_pairs={{1,0},{2,1},{3,2},{4,3},{5,4},{6,5},{7,6},{8,7},{9,8},{10,9},{11,1... | collective-permute-start | bytes 933896 | tf_op jit(solution)/shard_map/ppermute | solution.py:390
  11.9 3.0 %collective-permute-start = (f32[16,4864]{1,0:T(8,128)S(1)}, f32[16,4864]{1,0:T(8,128)S(1)}, u32[]{:S(2)}, u32[]{:S(2)}) collective-permute-start(f32[16,4864]{1,0:T(8,128)S(1)} %constant_dynamic-update-slice_fusion), channel_id=1, source_target_pairs={{0,1},{1,2},{2,3},{3,4},{4,5},{5,6},{6,7},{7,8},{8,9},{9,10},{10,1... | collective-permute-start | bytes 933896 | tf_op jit(solution)/shard_map/ppermute | solution.py:390
  15.0 3.1 %shard_map.96 = (bf16[16,512,256]{2,1,0:T(8,128)(2,1)S(1)}, f32[16,4096]{1,0:T(8,128)S(1)}) custom-call(f32[16,4096]{1,0:T(8,128)S(1)} %get-tuple-element.14.charges_ref.own_ref, f32[16,768]{1,0:T(8,128)S(1)} %get-tuple-element.15.centroid_ref.own_centroid_ref), custom_call_target="tpu_custom_call" | custom-call | tf_op jit(solution)/shard_map/pallas_call | solution.py:351
  18.1 0.0 copy-start.2
  18.1 1.9 %copy-done.2 = bf16[16,512,256]{2,1,0:T(8,128)(2,1)} copy-done((bf16[16,512,256]{2,1,0:T(8,128)(2,1)}, bf16[16,512,256]{2,1,0:T(8,128)(2,1)S(1)}, u32[]{:S(2)}) %copy-start.2) | copy-done | bytes 4194328
  20.0 0.8 copy.14.near_ref
  20.8 0.1 reshape.19
  20.9 0.0 copy-start.3
  20.9 23.2 %all-gather = f32[384,512]{1,0:T(8,128)S(1)} all-gather(f32[24,512]{1,0:T(8,128)S(1)} %get-tuple-element.18), channel_id=2, replica_groups=mesh['jobs'=2,'clus'=16] {'clus'}, dimensions={0}, use_global_device_ids=true | all-gather | bytes 835584 | tf_op jit(solution)/shard_map/all_gather | solution.py:394
  44.1 0.0 collective-permute-done.1
  44.1 0.0 collective-permute-done
  44.2 13.8 %shard_map.97 = (bf16[50,512,256]{2,1,0:T(8,128)(2,1)}, f32[16,4096]{1,0:T(8,128)S(1)}) custom-call(s32[1]{0:T(128)} %bitcast.1.base_ref, s32[16,4]{1,0:T(8,128)S(1)} %copy.14.near_ref, f32[16,4096]{1,0:T(8,128)S(1)} %get-tuple-element.14.charges_ref.own_ref, f32[16,4096]{1,0:T(8,128)S(1)} %slice.24.left_ref, f32[16,4096]{1,0:T(8,128)S(1)} %slice.25.right_ref, ...), custom_call_target="tpu_custom_call" | custom-call | tf_op jit(solution)/shard_map/pallas_call | solution.py:351
  57.9 0.0 copy-done.8
  57.9 0.0 copy-done.1
  57.9 0.0 copy-done.5
  58.0 0.0 copy-done.7
  58.0 0.0 copy-done.10
  58.0 11.7 %shard_map.98 = (f32[16,4096]{1,0:T(8,128)S(1)}, f32[16,4096]{1,0:T(8,128)S(1)}, f32[16,640]{1,0:T(8,128)S(1)}, bf16[16,64,1024]{2,1,0:T(8,128)(2,1)S(1)}) custom-call(s32[1]{0:T(128)} %bitcast.position_ref, s32[16,32]{1,0:T(8,128)S(1)} %copy-done.8, f32[16,24,512]{2,1,0:T(8,128)S(1)} %bitcast.9, f32[16,8,1]{2,1,0:T(8,128)S(1)} %bitcast.11, ...), custom_call_target="tpu_custom_call" | custom-call | tf_op jit(solution)/shard_map/pallas_call | solution.py:351
  69.7 1.9 %collective-permute-start.3 = (f32[16,4096]{1,0:T(8,128)S(1)}, f32[16,4096]{1,0:T(8,128)S(1)}, u32[]{:S(2)}, u32[]{:S(2)}) collective-permute-start(f32[16,4096]{1,0:T(8,128)S(1)} %get-tuple-element.21.charges_ref.own_ref), channel_id=1, source_target_pairs={{1,0},{2,1},{3,2},{4,3},{5,4},{6,5},{7,6},{8,7},{9,8},{10,9},{11,1... | collective-permute-start | bytes 786440 | tf_op jit(solution)/shard_map/ppermute | solution.py:390
  71.6 3.6 %collective-permute-start.2 = (f32[16,4096]{1,0:T(8,128)S(1)}, f32[16,4096]{1,0:T(8,128)S(1)}, u32[]{:S(2)}, u32[]{:S(2)}) collective-permute-start(f32[16,4096]{1,0:T(8,128)S(1)} %get-tuple-element.21.charges_ref.own_ref), channel_id=1, source_target_pairs={{0,1},{1,2},{2,3},{3,4},{4,5},{5,6},{6,7},{7,8},{8,9},{9,10},{10,1... | collective-permute-start | bytes 786440 | tf_op jit(solution)/shard_map/ppermute | solution.py:390
  75.2 0.0 copy-done.3
  75.3 1.3 %shard_map.99.start_ref = f32[16,4096]{1,0:T(8,128)S(1)} custom-call(f32[16,4096]{1,0:T(8,128)S(1)} %get-tuple-element.21.charges_ref.own_ref, bf16[16,512,256]{2,1,0:T(8,128)(2,1)S(1)} %copy-done.3), custom_call_target="tpu_custom_call" | custom-call | tf_op jit(solution)/shard_map/pallas_call | solution.py:351
  76.5 19.2 %all-gather.1 = f32[256,640]{1,0:T(8,128)S(1)} all-gather(f32[16,640]{1,0:T(8,128)S(1)} %get-tuple-element.23), channel_id=3, replica_groups=mesh['jobs'=2,'clus'=16] {'clus'}, dimensions={0}, use_global_device_ids=true | all-gather | bytes 696320 | tf_op jit(solution)/shard_map/all_gather | solution.py:427
  95.8 0.0 collective-permute-done.3.right_ref
  95.8 0.0 collective-permute-done.2.left_ref
  95.8 23.2 %shard_map.100 = (f32[16,4096]{1,0:T(8,128)}, f32[16,4096]{1,0:T(8,128)}) custom-call(s32[1]{0:T(128)} %bitcast.position_ref, s32[1]{0:T(128)} %bitcast.1.base_ref, s32[16,4]{1,0:T(8,128)S(1)} %copy.14.near_ref, s32[16,32]{1,0:T(8,128)S(1)} %copy-done.8, bf16[50,512,256]{2,1,0:T(8,128)(2,1)} %get-tuple-element.17.blocks_ref, ...), custom_call_target="tpu_custom_call" | custom-call | tf_op jit(solution)/shard_map/pallas_call | solution.py:351
  (8 shorter events, 0.1 us)
Async XLA Ops:
  0.6 57.3 %copy-start.8 = (s32[16,32]{1,0:T(8,128)S(1)}, s32[16,32]{1,0:T(8,128)}, u32[]{:S(2)}) copy-start(s32[16,32]{1,0:T(8,128)} %far_ref.3) | copy-start | bytes 6148
  0.6 1.0 copy-start
  1.7 0.9 copy-start.4
  2.6 0.8 copy-start.6
  3.5 0.8 copy-start.9
  4.2 53.7 %copy-start.1 = (f32[32,4096]{1,0:T(8,128)S(1)}, f32[32,4096]{1,0:T(8,128)}, u32[]{:S(2)}) copy-start(f32[32,4096]{1,0:T(8,128)} %basis_ref.5) | copy-start | bytes 1572868
  4.2 53.7 %copy-start.5 = (f32[16,4096]{1,0:T(8,128)S(1)}, f32[16,4096]{1,0:T(8,128)}, u32[]{:S(2)}) copy-start(f32[16,4096]{1,0:T(8,128)} %krylov_ref.5) | copy-start | bytes 786436
  4.2 53.7 %copy-start.7 = (f32[3,32,128]{2,1,0:T(8,128)S(1)}, f32[3,32,128]{2,1,0:T(8,128)}, u32[]{:S(2)}) copy-start(f32[3,32,128]{2,1,0:T(8,128)} %constant.15.clone.upright_ref) | copy-start | bytes 147460
  4.2 53.7 %copy-start.10 = (f32[8,128]{1,0:T(8,128)S(1)}, f32[8,128]{1,0:T(8,128)}, u32[]{:S(2)}) copy-start(f32[8,128]{1,0:T(8,128)} %constant.16.clone.flat_ref) | copy-start | bytes 12292
  9.3 34.8 %collective-permute-start.1 = (f32[16,4864]{1,0:T(8,128)S(1)}, f32[16,4864]{1,0:T(8,128)S(1)}, u32[]{:S(2)}, u32[]{:S(2)}) collective-permute-start(f32[16,4864]{1,0:T(8,128)S(1)} %constant_dynamic-update-slice_fusion), channel_id=1, source_target_pairs={{1,0},{2,1},{3,2},{4,3},{5,4},{6,5},{7,6},{8,7},{9,8},{10,9},{11,1... | collective-permute-start | bytes 933896 | tf_op jit(solution)/shard_map/ppermute | solution.py:390
  11.9 32.2 %collective-permute-start = (f32[16,4864]{1,0:T(8,128)S(1)}, f32[16,4864]{1,0:T(8,128)S(1)}, u32[]{:S(2)}, u32[]{:S(2)}) collective-permute-start(f32[16,4864]{1,0:T(8,128)S(1)} %constant_dynamic-update-slice_fusion), channel_id=1, source_target_pairs={{0,1},{1,2},{2,3},{3,4},{4,5},{5,6},{6,7},{7,8},{8,9},{9,10},{10,1... | collective-permute-start | bytes 933896 | tf_op jit(solution)/shard_map/ppermute | solution.py:390
  18.1 1.9 %copy-start.2 = (bf16[16,512,256]{2,1,0:T(8,128)(2,1)}, bf16[16,512,256]{2,1,0:T(8,128)(2,1)S(1)}, u32[]{:S(2)}) copy-start(bf16[16,512,256]{2,1,0:T(8,128)(2,1)S(1)} %get-tuple-element.22.blocks_ref) | copy-start | bytes 12582916
  20.9 54.3 %copy-start.3 = (bf16[16,512,256]{2,1,0:T(8,128)(2,1)S(1)}, bf16[16,512,256]{2,1,0:T(8,128)(2,1)}, u32[]{:S(2)}) copy-start(bf16[16,512,256]{2,1,0:T(8,128)(2,1)} %copy-done.2) | copy-start | bytes 12582916
  69.7 26.1 %collective-permute-start.3 = (f32[16,4096]{1,0:T(8,128)S(1)}, f32[16,4096]{1,0:T(8,128)S(1)}, u32[]{:S(2)}, u32[]{:S(2)}) collective-permute-start(f32[16,4096]{1,0:T(8,128)S(1)} %get-tuple-element.21.charges_ref.own_ref), channel_id=1, source_target_pairs={{1,0},{2,1},{3,2},{4,3},{5,4},{6,5},{7,6},{8,7},{9,8},{10,9},{11,1... | collective-permute-start | bytes 786440 | tf_op jit(solution)/shard_map/ppermute | solution.py:390
  71.6 24.2 %collective-permute-start.2 = (f32[16,4096]{1,0:T(8,128)S(1)}, f32[16,4096]{1,0:T(8,128)S(1)}, u32[]{:S(2)}, u32[]{:S(2)}) collective-permute-start(f32[16,4096]{1,0:T(8,128)S(1)} %get-tuple-element.21.charges_ref.own_ref), channel_id=1, source_target_pairs={{0,1},{1,2},{2,3},{3,4},{4,5},{5,6},{6,7},{7,8},{8,9},{9,10},{10,1... | collective-permute-start | bytes 786440 | tf_op jit(solution)/shard_map/ppermute | solution.py:390

commit v2 on v0

v2 whole, which is shorter than its diff:
```python
import functools

import jax
import jax.numpy as jnp
import numpy as np
from jax import lax
from jax.experimental import pallas as pl
from jax.experimental.pallas import tpu as pltpu
from jax.sharding import PartitionSpec as P

REACH = 4
SMOOTHING = 0.04
COULOMB = 2.0
PROXY_RADIUS = 0.6
LANES = 128
F32 = jnp.float32
BF16 = jnp.bfloat16


def proxy_offsets(points):
    counter = np.arange(points, dtype=np.float32)
    height = 1.0 - (2.0 * counter + 1.0) / points
    radial = np.sqrt(1.0 - height * height)
    azimuth = counter * 2.399963
    return PROXY_RADIUS * np.stack([radial * np.cos(azimuth), radial * np.sin(azimuth), height]).astype(np.float32)


def split(value):
    high = value.astype(BF16)
    return high, (value - high.astype(F32)).astype(BF16)


def stacked(value):
    return jnp.concatenate(split(value), axis=0)


def folded(value):
    half = value.shape[0] // 2
    return value[:half] + value[half:]


def dot_nt(left, right):
    return lax.dot_general(left, right, (((1,), (1,)), ((), ())), preferred_element_type=F32)


def dot_nn(left, right):
    return lax.dot_general(left, right, (((1,), (0,)), ((), ())), preferred_element_type=F32)


def moments_of(weighted, basis_block):
    pieces = stacked(weighted)
    high, low = split(basis_block)
    return folded(dot_nt(pieces, high) + dot_nt(pieces, low))


def prepare_kernel(cl, vcl, rank, base_ref, vertices_hbm, corners_hbm, krylov_hbm, basis_hbm, payload_ref, area_ref, center_ref,
                   vertices_ref, corners_ref, krylov_ref, basis_ref, mesh_ref, local_ref, sems):
    moves = [
        pltpu.make_async_copy(source, target, sems.at[i])
        for i, (source, target) in enumerate(((vertices_hbm, vertices_ref), (corners_hbm, corners_ref), (krylov_hbm, krylov_ref), (basis_hbm, basis_ref)))
    ]
    for move in moves:
        move.start()
    rhs, panels = krylov_ref.shape
    clusters = panels // cl
    parts = cl // LANES
    moves[0].wait()
    for c in range(clusters):
        mesh_ref[3 * c:3 * c + 3, :] = vertices_ref[:, c * vcl:(c + 1) * vcl]
    moves[1].wait()
    for i in range(clusters * parts):
        local_ref[3 * i:3 * i + 3, :] = corners_ref[:, i * LANES:(i + 1) * LANES]
    first = base_ref[0] + vcl * lax.broadcasted_iota(jnp.int32, (clusters, LANES), 0)
    tables = [mesh_ref[pl.ds(k, clusters, stride=3), :] for k in range(3)]
    sums = [None] * 3
    for h in range(parts):
        local = [local_ref[pl.ds(3 * h + m, clusters, stride=3 * parts), :] - first for m in range(3)]
        corner = [[jnp.take_along_axis(tables[k], local[m], axis=1, mode="promise_in_bounds") for k in range(3)] for m in range(3)]
        for k in range(3):
            middle = (corner[0][k] + corner[1][k] + corner[2][k]) / 3.0
            payload_ref[:, panels + k * cl + h * LANES:panels + k * cl + (h + 1) * LANES] = middle
            sums[k] = middle if h == 0 else sums[k] + middle
        one = [corner[1][k] - corner[0][k] for k in range(3)]
        two = [corner[2][k] - corner[0][k] for k in range(3)]
        normal = [one[1] * two[2] - one[2] * two[1], one[2] * two[0] - one[0] * two[2], one[0] * two[1] - one[1] * two[0]]
        area_ref[:, h * LANES:(h + 1) * LANES] = 0.5 * jnp.sqrt(normal[0] * normal[0] + normal[1] * normal[1] + normal[2] * normal[2])
    table = panels + 3 * cl
    span = clusters * rank
    mine = lax.broadcasted_iota(jnp.int32, (clusters, span), 1) // rank == lax.broadcasted_iota(jnp.int32, (clusters, span), 0)
    half = span // 2
    payload_ref[:, table + span:] = jnp.zeros_like(payload_ref[:, table + span:])
    for k in range(3):
        center = jnp.sum(sums[k], axis=1, keepdims=True) / cl
        center_ref[:, k * LANES:(k + 1) * LANES] = jnp.broadcast_to(center, (clusters, LANES))
        row = jnp.sum(jnp.where(mine, center, 0.0), axis=0, keepdims=True)
        payload_ref[k:k + 1, table + span:] = row[:, 0:half]
        payload_ref[8 + k:9 + k, table + span:] = row[:, half:]
    moves[2].wait()
    moves[3].wait()
    for c in range(clusters):
        lanes = slice(c * cl, (c + 1) * cl)
        charges = area_ref[c:c + 1, :] * krylov_ref[:, lanes]
        payload_ref[:, lanes] = charges
        payload_ref[:, table + c * rank:table + (c + 1) * rank] = moments_of(charges, basis_ref[:, lanes])


def columns_of(payload_ref, panels, c, cl, columns_ref, at):
    rows = [payload_ref[c:c + 1, panels + k * cl:panels + (k + 1) * cl] for k in range(3)]
    upright = jnp.transpose(jnp.concatenate(rows * 2 + rows[:2], axis=0))
    for k in range(3):
        columns_ref[at, k] = jnp.broadcast_to(upright[:, k:k + 1], (cl, LANES))


def near_block(columns, source, cl, out_ref, at):
    for h in range(cl // LANES):
        lanes = slice(h * LANES, (h + 1) * LANES)
        gap = [columns[k] - source(k, h) for k in range(3)]
        square = gap[0] * gap[0] + gap[1] * gap[1] + gap[2] * gap[2]
        high, low = split(lax.rsqrt(square + SMOOTHING))
        out_ref[at, 0:cl, lanes] = high
        out_ref[at, cl:2 * cl, lanes] = low


def near_product(pieces, block_ref, at, cl):
    return dot_nt(pieces, block_ref[at, 0:cl, :]) + dot_nt(pieces, block_ref[at, cl:2 * cl, :])


def self_kernel(cl, payload_ref, blocks_ref, near_ref, columns_ref):
    panels = near_ref.shape[1]
    for c in range(panels // cl):
        columns_of(payload_ref, panels, c, cl, columns_ref, c % 2)
        source = lambda k, h: payload_ref[c:c + 1, panels + k * cl + h * LANES:panels + k * cl + (h + 1) * LANES]
        near_block([columns_ref[c % 2, k] for k in range(3)], source, cl, blocks_ref, c)
        lanes = slice(c * cl, (c + 1) * cl)
        near_ref[:, lanes] = folded(near_product(stacked(payload_ref[:, lanes]), blocks_ref, c, cl))


def self_again_kernel(cl, payload_ref, blocks_ref, near_ref):
    for c in range(near_ref.shape[1] // cl):
        lanes = slice(c * cl, (c + 1) * cl)
        near_ref[:, lanes] = folded(near_product(stacked(payload_ref[:, lanes]), blocks_ref, c, cl))


def fill_charges(pieces_ref, blocks, clusters, cl):
    for b, ref in enumerate(blocks):
        for c in range(clusters):
            pieces_ref[b * clusters + c] = stacked(ref[:, c * cl:(c + 1) * cl])
    pieces_ref[3 * clusters] = jnp.zeros_like(pieces_ref[3 * clusters])


def list_pairs(near_ref, base, list_ref, pad):
    slots, clusters = near_ref.shape
    n = jnp.int32(0)
    for c in range(clusters):
        for k in range(1, slots):
            j = near_ref[k, c]
            list_ref[0, n] = jnp.int32(c)
            list_ref[1, n] = j - base
            list_ref[2, n] = n
            n = n + (j >= 0).astype(jnp.int32)
    for i in range(pad):
        list_ref[0, n + i] = jnp.int32(0)
        list_ref[1, n + i] = jnp.int32(3 * clusters)
        list_ref[2, n + i] = jnp.int32(0)
    return n


def remote_kernel(cl, base_ref, near_ref, own_ref, left_ref, right_ref, start_ref, even_ref, odd_ref, near_out_ref,
                  pieces_ref, sources_ref, columns_ref, total_ref, list_ref):
    panels = start_ref.shape[1]
    clusters = panels // cl
    count = list_pairs(near_ref, base_ref[0], list_ref, 2)
    sources_ref[3 * clusters] = jnp.zeros_like(sources_ref[3 * clusters])
    for b, ref in enumerate((left_ref, own_ref, right_ref)):
        for c in range(clusters):
            for k in range(3):
                sources_ref[b * clusters + c, k:k + 1, :] = ref[c:c + 1, panels + k * cl:panels + (k + 1) * cl]
    fill_charges(pieces_ref, (left_ref, own_ref, right_ref), clusters, cl)
    for c in range(clusters):
        columns_of(own_ref, panels, c, cl, columns_ref, c)
        total_ref[c] = jnp.zeros_like(total_ref[c])
    odd_ref[0] = jnp.zeros_like(odd_ref[0])
    steps = (count + 1) // 2

    def build(ref, at, i):
        c, j = list_ref[0, i], list_ref[1, i]
        source = lambda k, h: sources_ref[j, k:k + 1, h * LANES:(h + 1) * LANES]
        near_block([columns_ref[c, k] for k in range(3)], source, cl, ref, at)

    def product(ref, at, i):
        return near_product(pieces_ref[list_ref[1, i]], ref, at, cl)

    def step(m, _):
        before = jnp.maximum(2 * m - 1, 0)
        part = product(odd_ref, m, before)
        build(even_ref, m, 2 * m)
        total_ref[list_ref[0, before]] += part
        part = product(even_ref, m, 2 * m)
        build(odd_ref, m + 1, 2 * m + 1)
        total_ref[list_ref[0, 2 * m]] += part
        return 0

    lax.fori_loop(0, steps, step, 0)
    last = jnp.maximum(2 * steps - 1, 0)
    total_ref[list_ref[0, last]] += product(odd_ref, steps, last)
    for c in range(clusters):
        lanes = slice(c * cl, (c + 1) * cl)
        near_out_ref[:, lanes] = start_ref[:, lanes] + folded(total_ref[c])


def remote_again_kernel(cl, base_ref, near_ref, own_ref, left_ref, right_ref, start_ref, even_ref, odd_ref, near_out_ref, pieces_ref, total_ref, list_ref):
    clusters = start_ref.shape[1] // cl
    count = list_pairs(near_ref, base_ref[0], list_ref, 4)
    fill_charges(pieces_ref, (left_ref, own_ref, right_ref), clusters, cl)
    for c in range(clusters):
        total_ref[c] = jnp.zeros_like(total_ref[c])

    def step(m, _):
        parts = []
        for w in range(4):
            i = 4 * m + w
            at = list_ref[2, i]
            parts.append(near_product(pieces_ref[list_ref[1, i]], (even_ref, odd_ref)[w % 2], at // 2 + w % 2, cl))
        for w in range(4):
            total_ref[list_ref[0, 4 * m + w]] += parts[w]
        return 0

    lax.fori_loop(0, (count + 3) // 4, step, 0)
    for c in range(clusters):
        lanes = slice(c * cl, (c + 1) * cl)
        near_out_ref[:, lanes] = start_ref[:, lanes] + folded(total_ref[c])


def window_tiles(tables, clusters, rank):
    groups = clusters * rank // LANES
    width = tables[0].shape[1] // 3
    for side, ref in enumerate(tables):
        for b in range(3):
            for g in range(groups):
                yield (side * 3 + b) * groups + g, ref, b * width, g


def load_window(tables, clusters, rank, pieces_ref, middle_ref):
    rhs = pieces_ref.shape[1] // 2
    per = LANES // rank
    span = clusters * rank
    count = pieces_ref.shape[0] // per
    for at, ref, first, g in window_tiles(tables, clusters, rank):
        tile = ref[:, first + g * LANES:first + (g + 1) * LANES]
        for s in range(per):
            pieces_ref[s * count + at] = stacked(pltpu.roll(tile, s * rank, 1) if s else tile)
        if middle_ref is not None:
            half = span // 2 // LANES
            row, lane = 8 * (g // half), first + span + g % half * LANES
            tile = ref[row:row + 8, lane:lane + LANES]
            for s in range(per):
                middle_ref[s * count + at] = pltpu.roll(tile, s * rank, 1) if s else tile


def pick(source_ref, at_ref, c, g, per, lane):
    row = None
    for u in range(per):
        take = source_ref[at_ref[c, g * per + u]]
        row = take if row is None else jnp.where(lane == u, take, row)
    return row


def far_fields(gathered_ref, coupling_ref, fields_ref, rank):
    for c in range(gathered_ref.shape[0]):
        field = folded(dot_nt(gathered_ref[c], coupling_ref[c]))
        fields_ref[c] = stacked(field[:, 0:rank] + field[:, rank:2 * rank])


def far_potential(field, basis_block):
    high, low = split(basis_block)
    return folded(dot_nn(field, high) + dot_nn(field, low))


def image_kernel(cl, rank, at_ref, below_ref, above_ref, center_ref, basis_ref, area_ref, near_ref, krylov_ref, upright_ref, flat_ref,
                 image_ref, payload_ref, coupling_ref, pieces_ref, middle_ref, gathered_ref, fields_ref):
    rhs, panels = krylov_ref.shape
    clusters = panels // cl
    span = clusters * rank
    per = LANES // rank
    load_window((below_ref, above_ref), clusters, rank, pieces_ref, middle_ref)
    lane = lax.broadcasted_iota(jnp.int32, (1, LANES), 1) // rank
    for c in range(clusters):
        mine = [flat_ref[k:k + 1, :] - center_ref[c:c + 1, k * LANES:(k + 1) * LANES] for k in range(3)]
        for g in range(at_ref.shape[1] // per):
            lanes = slice(g * LANES, (g + 1) * LANES)
            gathered_ref[c, :, lanes] = pick(pieces_ref, at_ref, c, g, per, lane)
            center = pick(middle_ref, at_ref, c, g, per, lane)
            gap = [(center[k:k + 1] + mine[k]) - upright_ref[k] for k in range(3)]
            high, low = split(lax.rsqrt(gap[0] * gap[0] + gap[1] * gap[1] + gap[2] * gap[2] + SMOOTHING))
            coupling_ref[c, 0:rank, lanes] = high
            coupling_ref[c, rank:2 * rank, lanes] = low
    far_fields(gathered_ref, coupling_ref, fields_ref, rank)
    squared = correlation = jnp.zeros((rhs, cl), F32)
    for c in range(clusters):
        lanes = slice(c * cl, (c + 1) * cl)
        area = area_ref[c:c + 1, :]
        image = COULOMB * area * (near_ref[:, lanes] + far_potential(fields_ref[c], basis_ref[:, lanes]))
        image_ref[:, lanes] = image
        payload_ref[:, lanes] = area * image
        krylov = krylov_ref[:, lanes]
        squared = squared + krylov * krylov
        correlation = correlation + krylov * image
    for c in range(clusters):
        lanes = slice(c * cl, (c + 1) * cl)
        payload_ref[:, panels + c * rank:panels + (c + 1) * rank] = moments_of(payload_ref[:, lanes], basis_ref[:, lanes])
    squared = jnp.sum(squared, axis=1, keepdims=True)
    correlation = jnp.sum(correlation, axis=1, keepdims=True)
    local = ratio(correlation, squared)
    residual = image_ref[...] - local * krylov_ref[...]
    payload_ref[:, panels + span:] = in_lanes(squared, correlation, jnp.sum(residual * residual, axis=1, keepdims=True), local)


def ratio(correlation, squared):
    return jnp.where(squared > 0, correlation / jnp.where(squared > 0, squared, 1.0), 0.0)


def in_lanes(*columns):
    lane = lax.broadcasted_iota(jnp.int32, (columns[0].shape[0], LANES), 1)
    out = columns[-1]
    for i, column in enumerate(columns[:-1]):
        out = jnp.where(lane == i, column, out)
    return out


def merged(groups):
    squared = sum(group[:, 0:1] for group in groups)
    correlation = sum(group[:, 1:2] for group in groups)
    local = ratio(correlation, squared)
    energy = 0.0
    for group in groups:
        gap = local - group[:, 3:4]
        energy = energy + (group[:, 2:3] + gap * gap * group[:, 0:1])
    return squared, correlation, energy, local


def window_sums_kernel(at, *refs):
    own_ref, left_ref, right_ref, below_ref, above_ref, out_ref = refs
    width = below_ref.shape[1] // 3
    groups = [ref[:, ref.shape[1] - LANES:] for ref in (own_ref, left_ref, right_ref)]
    groups += [below_ref[:, (b + 1) * width - LANES:(b + 1) * width] for b in range(3)]
    groups += [above_ref[:, (b + 1) * width - LANES:(b + 1) * width] for b in range(2)]
    out_ref[...] = in_lanes(*merged(groups))


def double_sums_kernel(one_ref, two_ref, out_ref):
    out_ref[...] = in_lanes(*merged([one_ref[...], two_ref[...]]))


def far_again_kernel(cl, rank, at_ref, below_ref, above_ref, coupling_ref, basis_ref, area_ref, near_ref, image_ref, pieces_ref, gathered_ref, fields_ref):
    clusters = near_ref.shape[1] // cl
    per = LANES // rank
    load_window((below_ref, above_ref), clusters, rank, pieces_ref, None)
    lane = lax.broadcasted_iota(jnp.int32, (1, LANES), 1) // rank
    for c in range(clusters):
        for g in range(at_ref.shape[1] // per):
            gathered_ref[c, :, g * LANES:(g + 1) * LANES] = pick(pieces_ref, at_ref, c, g, per, lane)
    far_fields(gathered_ref, coupling_ref, fields_ref, rank)
    for c in range(clusters):
        lanes = slice(c * cl, (c + 1) * cl)
        image_ref[:, lanes] = COULOMB * area_ref[c:c + 1, :] * (near_ref[:, lanes] + far_potential(fields_ref[c], basis_ref[:, lanes]))


def finish_kernel(total, one_ref, two_ref, krylov_ref, image_ref, again_ref, next_ref, second_ref):
    squared, correlation, energy, local = merged([one_ref[...], two_ref[...]])
    projection = correlation / (squared + 1e-06)
    gap = projection - local
    scaling = 1.0 / jnp.sqrt((energy + gap * gap * squared) / total + 1e-06)
    image = image_ref[...]
    next_ref[...] = (image - projection * krylov_ref[...]) * scaling
    second_ref[...] = (again_ref[...] - projection * image) * scaling


def call(kernel, outs, scratch, memory, *args, limit=24):
    spaces = {"s": pltpu.SMEM, "v": pltpu.VMEM, "a": pl.ANY, "h": pltpu.HBM}
    ins, out_spaces = memory.split(">")
    return pl.pallas_call(
        kernel,
        out_shape=[jax.ShapeDtypeStruct(*out) for out in outs],
        in_specs=[pl.BlockSpec(memory_space=spaces[m]) for m in ins],
        out_specs=[pl.BlockSpec(memory_space=spaces[m]) for m in out_spaces],
        scratch_shapes=scratch,
        compiler_params=pltpu.CompilerParams(vmem_limit_bytes=limit * 2 ** 20),
    )(*args)


def body(vertices, panel_vertices, near_pairs, far_pairs, basis, krylov):
    clusters, slots = near_pairs.shape
    partners = far_pairs.shape[1]
    rhs, panels = krylov.shape
    rank = basis.shape[0]
    cl = panels // clusters
    vcl = vertices.shape[1] // clusters
    span = clusters * rank
    per = LANES // rank
    devices = lax.axis_size("clus")
    position = lax.axis_index("clus")
    base = ((position - 1) * clusters).reshape(1).astype(jnp.int32)
    corner_base = (position * vertices.shape[1]).reshape(1).astype(jnp.int32)
    offsets = proxy_offsets(rank)
    upright = jnp.asarray(np.ascontiguousarray(np.broadcast_to(offsets[:, :, None], (3, rank, LANES))))
    flat = jnp.asarray(np.concatenate([np.tile(offsets, (1, per)), np.zeros((5, LANES), np.float32)]))
    live = clusters * (slots - 1)
    half = ((live + 1) // 2 + 1, 2 * cl, cl)
    near_lists = near_pairs.T
    step = far_pairs // clusters - position
    block = jnp.where(step < 0, step + REACH, step + REACH - 3)
    turn = (jnp.arange(partners, dtype=jnp.int32) - far_pairs) % per
    tiles = 6 * span // LANES
    at = turn * tiles + block * (span // LANES) + far_pairs % clusters // per

    def shifted(value, steps):
        return lax.ppermute(value, "clus", [(i, (i + steps) % devices) for i in range(devices)])

    def relayed(own, left, right, first):
        triple = jnp.concatenate([value[:, first:] for value in (left, own, right)], axis=1)
        return shifted(triple, 3), shifted(triple, -3)

    table = panels + 3 * cl
    payload, area, centers = call(
        functools.partial(prepare_kernel, cl, vcl, rank),
        [((rhs, table + span + span // 2), F32), ((clusters, cl), F32), ((clusters, 3 * LANES), F32)],
        [
            pltpu.VMEM(vertices.shape, F32),
            pltpu.VMEM(panel_vertices.shape, jnp.int32),
            pltpu.VMEM(krylov.shape, F32),
            pltpu.VMEM(basis.shape, F32),
            pltpu.VMEM((3 * clusters, vcl), F32),
            pltpu.VMEM((3 * panels // LANES, LANES), jnp.int32),
            pltpu.SemaphoreType.DMA((4,)),
        ],
        "shhhh>vvv",
        corner_base, vertices, panel_vertices, krylov, basis,
    )
    left, right = shifted(payload, 1), shifted(payload, -1)
    own_blocks, near = call(
        functools.partial(self_kernel, cl),
        [((clusters, 2 * cl, cl), BF16), ((rhs, panels), F32)],
        [pltpu.VMEM((2, 3, cl, LANES), F32)],
        "v>vv",
        payload,
    )
    below, above = relayed(payload, left, right, table)
    pieces = pltpu.VMEM((3 * clusters + 1, 2 * rhs, cl), BF16)
    total = pltpu.VMEM((clusters, 2 * rhs, cl), F32)
    pairs = pltpu.SMEM((3, live + 4), jnp.int32)
    even, odd, near = call(
        functools.partial(remote_kernel, cl),
        [(half, BF16), (half, BF16), ((rhs, panels), F32)],
        [pieces, pltpu.VMEM((3 * clusters + 1, 8, cl), F32), pltpu.VMEM((clusters, 3, cl, LANES), F32), total, pairs],
        "ssvvvv>vvv",
        base, near_lists, payload, left, right, near,
    )
    window = pltpu.VMEM((per * tiles, 2 * rhs, LANES), BF16)
    gathered = pltpu.VMEM((clusters, 2 * rhs, partners * rank), BF16)
    fields = pltpu.VMEM((clusters, 2 * rhs, rank), BF16)
    image, payload, coupling = call(
        functools.partial(image_kernel, cl, rank),
        [((rhs, panels), F32), ((rhs, panels + span + LANES), F32), ((clusters, 2 * rank, partners * rank), BF16)],
        [window, pltpu.VMEM((per * tiles, 8, LANES), F32), gathered, fields],
        "svvvvvvvvv>vvv",
        at, below, above, centers, basis, area, near, krylov, upright, flat,
    )
    left, right = shifted(payload, 1), shifted(payload, -1)
    (near,) = call(functools.partial(self_again_kernel, cl), [((rhs, panels), F32)], [], "vv>v", payload, own_blocks)
    below, above = relayed(payload, left, right, panels)
    (near,) = call(
        functools.partial(remote_again_kernel, cl),
        [((rhs, panels), F32)],
        [pieces, total, pairs],
        "ssvvvvvv>v",
        base, near_lists, payload, left, right, near, even, odd,
    )
    sums_shape = [((rhs, LANES), F32)]
    (sums,) = call(functools.partial(window_sums_kernel, panels), sums_shape, [], "vvvvv>v", payload, left, right, below, above)
    size = 2 * REACH
    other = shifted(sums, size)
    while 2 * size < devices:
        (sums,) = call(double_sums_kernel, sums_shape, [], "vv>v", sums, other)
        size = 2 * size
        other = shifted(sums, size)
    (again,) = call(
        functools.partial(far_again_kernel, cl, rank),
        [((rhs, panels), F32)],
        [window, gathered, fields],
        "svvvvvv>v",
        at, below, above, coupling, basis, area, near,
    )
    return tuple(call(
        functools.partial(finish_kernel, panels * devices),
        [((rhs, panels), F32), ((rhs, panels), F32)],
        [],
        "vvvvv>vv",
        sums, other, krylov, image, again,
    ))


def solution(mesh):
    whole = P(None, ("jobs", "clus"))
    rows = P(("jobs", "clus"), None)
    return jax.shard_map(
        body,
        mesh=mesh,
        in_specs=(whole, whole, rows, rows, whole, whole),
        out_specs=(whole, whole),
        check_vma=False,
    )
```

time: 273 us -> 69 us (0.25)
  the two profiles are of different devices: /device:TPU:13 before, /device:TPU:19 now
where the time goes in v2:
time: 69 us; the launch traced here: 67.7 us
  starting transfers between devices  20.3 us (29%)
  Pallas kernels  19.3 us (28%)
  waiting for transfers between devices  14.6 us (21%)
  local copies, waits for them, and re-layouts  11.9 us (17%)
  between operations  0.8 us (1%)
  other arithmetic  0.74 us (1%)
    ppermute x9, starting transfers between devices, shifted(): lax.ppermute(value, 'clus', [(i, (i + steps) % devices) for i in range(de...  20.3 us
    pallas_call x9, Pallas kernels, call(): pl.pallas_call(kernel, out_shape=[jax.ShapeDtypeStruct(*out) for out in o...  19.3 us
    ppermute x9, waiting for transfers between devices, shifted(): lax.ppermute(value, 'clus', [(i, (i + steps) % devices) for i in range(de...  14.6 us
    unnamed x28, local copies, waits for them, and re-layouts  11.9 us
  transfers between devices with their start and end apart: 9, of which 5 were waited for; matrix products, arithmetic and copies ran while one was open for 1% of the time, Pallas kernels for 20%

profile of v2, /device:TPU:19, one launch (start us, length us, event | category | flops | bytes accessed | tf_op | source)
XLA Modules:
  0.0 67.7 jit_solution(325495942151290138)
XLA Ops:
  0.6 0.0 copy-start.12
  0.6 0.0 copy-start
  0.7 1.0 %copy-done = f32[32,4096]{1,0:T(8,128)S(1)} copy-done((f32[32,4096]{1,0:T(8,128)S(1)}, f32[32,4096]{1,0:T(8,128)}, u32[]{:S(2)}) %copy-start) | copy-done | bytes 524312
  1.7 0.0 copy-start.5
  1.7 0.9 %copy-done.5 = f32[16,4096]{1,0:T(8,128)S(1)} copy-done((f32[16,4096]{1,0:T(8,128)S(1)}, f32[16,4096]{1,0:T(8,128)}, u32[]{:S(2)}) %copy-start.5) | copy-done | bytes 262168
  2.6 0.0 copy-start.8
  2.6 0.8 %copy-done.8 = s32[3,4096]{1,0:T(4,128)S(1)} copy-done((s32[3,4096]{1,0:T(4,128)S(1)}, s32[3,4096]{1,0:T(4,128)}, u32[]{:S(2)}) %copy-start.8) | copy-done | bytes 49176
  3.5 0.0 copy-start.10
  3.5 0.8 %copy-done.10 = f32[3,2048]{1,0:T(4,128)S(1)} copy-done((f32[3,2048]{1,0:T(4,128)S(1)}, f32[3,2048]{1,0:T(4,128)}, u32[]{:S(2)}) %copy-start.10) | copy-done | bytes 24600
  4.2 0.9 %shard_map.95 = (f32[16,5632]{1,0:T(8,128)S(1)}, f32[16,256]{1,0:T(8,128)S(1)}, f32[16,384]{1,0:T(8,128)S(1)}) custom-call(s32[1]{0:T(128)} %bitcast.base_ref, f32[3,2048]{1,0:T(4,128)S(1)} %copy-done.10, s32[3,4096]{1,0:T(4,128)S(1)} %copy-done.8, f32[16,4096]{1,0:T(8,128)S(1)} %copy-done.5, f32[32,4096]{1,0:T(8,128)S(1)} %copy-done), custom_call_target="tpu_custom_call" | custom-call | tf_op jit(solution)/shard_map/pallas_call | solution.py:381
  5.1 0.7 %collective-permute-start.1 = (f32[16,5632]{1,0:T(8,128)S(1)}, f32[16,5632]{1,0:T(8,128)S(1)}, u32[]{:S(2)}, u32[]{:S(2)}) collective-permute-start(f32[16,5632]{1,0:T(8,128)S(1)} %get-tuple-element.13.payload_ref.own_ref), channel_id=1, source_target_pairs={{0,15},{1,0},{2,1},{3,2},{4,3},{5,4},{6,5},{7,6},{8,7},{9,8},{10,9... | collective-permute-start | bytes 1081352 | tf_op jit(solution)/shard_map/ppermute | solution.py:417
  5.8 1.2 %collective-permute-start = (f32[16,5632]{1,0:T(8,128)S(1)}, f32[16,5632]{1,0:T(8,128)S(1)}, u32[]{:S(2)}, u32[]{:S(2)}) collective-permute-start(f32[16,5632]{1,0:T(8,128)S(1)} %get-tuple-element.13.payload_ref.own_ref), channel_id=1, source_target_pairs={{0,1},{1,2},{2,3},{3,4},{4,5},{5,6},{6,7},{7,8},{8,9},{9,10},{10,1... | collective-permute-start | bytes 1081352 | tf_op jit(solution)/shard_map/ppermute | solution.py:417
  7.0 3.1 %shard_map.96 = (bf16[16,512,256]{2,1,0:T(8,128)(2,1)S(1)}, f32[16,4096]{1,0:T(8,128)S(1)}) custom-call(f32[16,5632]{1,0:T(8,128)S(1)} %get-tuple-element.13.payload_ref.own_ref), custom_call_target="tpu_custom_call" | custom-call | tf_op jit(solution)/shard_map/pallas_call | solution.py:381
  10.2 0.0 copy-start.3
  10.2 2.0 %copy-done.3 = bf16[16,512,256]{2,1,0:T(8,128)(2,1)} copy-done((bf16[16,512,256]{2,1,0:T(8,128)(2,1)}, bf16[16,512,256]{2,1,0:T(8,128)(2,1)S(1)}, u32[]{:S(2)}) %copy-start.3) | copy-done | bytes 4194328
  12.1 3.8 %collective-permute-done.1.right_ref = f32[16,5632]{1,0:T(8,128)S(1)} collective-permute-done((f32[16,5632]{1,0:T(8,128)S(1)}, f32[16,5632]{1,0:T(8,128)S(1)}, u32[]{:S(2)}, u32[]{:S(2)}) %collective-permute-start.1) | collective-permute-done | bytes 360480 | tf_op jit(solution)/shard_map/ppermute | solution.py:417
  15.9 0.0 collective-permute-done.left_ref
  16.0 1.7 %collective-permute-start.3 = (f32[16,2304]{1,0:T(8,128)S(1)}, f32[16,2304]{1,0:T(8,128)S(1)}, u32[]{:S(2)}, u32[]{:S(2)}) collective-permute-start(f32[16,2304]{1,0:T(8,128)S(1)} %pad_maximum_fusion), channel_id=1, source_target_pairs={{0,13},{1,14},{2,15},{3,0},{4,1},{5,2},{6,3},{7,4},{8,5},{9,6},{10... | collective-permute-start | bytes 442376 | tf_op jit(solution)/shard_map/ppermute | solution.py:417
  17.7 0.1 collective-permute-start.2
  17.8 0.7 %fusion.3.at_ref = s32[16,32]{1,0:T(8,128)S(1)} fusion(s32[16,32]{1,0:T(8,128)} %param.11, s32[]{:T(128)S(6)} %axis_index.12), kind=kLoop, calls=%fused_computation.17 | loop fusion | flops 28160 | bytes 4100 | tf_op jit(solution)/shard_map/add | solution.py:414
  18.5 0.0 copy-start.11
  18.5 0.7 copy-done.11
  19.2 5.3 %shard_map.97 = (bf16[25,512,256]{2,1,0:T(8,128)(2,1)S(1)}, bf16[25,512,256]{2,1,0:T(8,128)(2,1)S(1)}, f32[16,4096]{1,0:T(8,128)S(1)}) custom-call(s32[1]{0:T(128)} %bitcast.1.base_ref, s32[4,16]{1,0:T(4,128)S(1)} %bitcast.3, f32[16,5632]{1,0:T(8,128)S(1)} %get-tuple-element.13.payload_ref.own_ref, f32[16,5632]{1,0:T(8,128)S(1)} %collective-permute-done.left_ref, ...), custom_call_target="tpu_custom_call" | custom-call | tf_op jit(solution)/shard_map/pallas_call | solution.py:381
  24.5 0.0 collective-permute-done.3.above_ref
  24.5 0.2 collective-permute-done.2.below_ref
  24.7 0.0 copy-start.1
  24.7 1.0 %copy-done.1 = f32[32,4096]{1,0:T(8,128)S(1)} copy-done((f32[32,4096]{1,0:T(8,128)S(1)}, f32[32,4096]{1,0:T(8,128)}, u32[]{:S(2)}) %copy-start.1) | copy-done | bytes 524312
  25.8 0.0 copy-start.6
  25.8 0.9 %copy-done.6 = f32[16,4096]{1,0:T(8,128)S(1)} copy-done((f32[16,4096]{1,0:T(8,128)S(1)}, f32[16,4096]{1,0:T(8,128)}, u32[]{:S(2)}) %copy-start.6) | copy-done | bytes 262168
  26.7 0.0 copy-start.9
  26.7 0.8 %copy-done.9 = f32[3,32,128]{2,1,0:T(8,128)S(1)} copy-done((f32[3,32,128]{2,1,0:T(8,128)S(1)}, f32[3,32,128]{2,1,0:T(8,128)}, u32[]{:S(2)}) %copy-start.9) | copy-done | bytes 49176
  27.5 0.0 copy-start.13
  27.5 0.7 %copy-done.13 = f32[8,128]{1,0:T(8,128)S(1)} copy-done((f32[8,128]{1,0:T(8,128)S(1)}, f32[8,128]{1,0:T(8,128)}, u32[]{:S(2)}) %copy-start.13) | copy-done | bytes 4120
  28.2 3.4 %shard_map.98 = (f32[16,4096]{1,0:T(8,128)S(1)}, f32[16,4736]{1,0:T(8,128)S(1)}, bf16[16,64,1024]{2,1,0:T(8,128)(2,1)S(1)}) custom-call(s32[16,32]{1,0:T(8,128)S(1)} %fusion.3.at_ref, f32[16,2304]{1,0:T(8,128)S(1)} %collective-permute-done.2.below_ref, f32[16,2304]{1,0:T(8,128)S(1)} %collective-permute-done.3.above_ref, ...), custom_call_target="tpu_custom_call" | custom-call | tf_op jit(solution)/shard_map/pallas_call | solution.py:381
  31.7 0.0 collective-permute-start.5
  31.7 8.2 %collective-permute-start.4 = (f32[16,4736]{1,0:T(8,128)S(1)}, f32[16,4736]{1,0:T(8,128)S(1)}, u32[]{:S(2)}, u32[]{:S(2)}) collective-permute-start(f32[16,4736]{1,0:T(8,128)S(1)} %get-tuple-element.18.refs_0_.payload_ref.own_ref), channel_id=1, source_target_pairs={{0,1},{1,2},{2,3},{3,4},{4,5},{5,6},{6,7},{7,8},{8,9},{9,10},{10,1... | collective-permute-start | bytes 909320 | tf_op jit(solution)/shard_map/ppermute | solution.py:417
  39.9 4.4 %collective-permute-done.5.refs_2_.right_ref = f32[16,4736]{1,0:T(8,128)S(1)} collective-permute-done((f32[16,4736]{1,0:T(8,128)S(1)}, f32[16,4736]{1,0:T(8,128)S(1)}, u32[]{:S(2)}, u32[]{:S(2)}) %collective-permute-start.5) | collective-permute-done | bytes 303136 | tf_op jit(solution)/shard_map/ppermute | solution.py:417
  44.3 0.0 collective-permute-done.4.refs_1_.left_ref
  44.3 0.1 collective-permute-start.7
  44.4 1.7 %collective-permute-start.6 = (f32[16,1920]{1,0:T(8,128)S(1)}, f32[16,1920]{1,0:T(8,128)S(1)}, u32[]{:S(2)}, u32[]{:S(2)}) collective-permute-start(f32[16,1920]{1,0:T(8,128)S(1)} %pad_maximum_fusion.1), channel_id=1, source_target_pairs={{0,3},{1,4},{2,5},{3,6},{4,7},{5,8},{6,9},{7,10},{8,11},{9,12},{10... | collective-permute-start | bytes 368648 | tf_op jit(solution)/shard_map/ppermute | solution.py:417
  46.1 2.6 %collective-permute-done.7.refs_4_.above_ref = f32[16,1920]{1,0:T(8,128)S(1)} collective-permute-done((f32[16,1920]{1,0:T(8,128)S(1)}, f32[16,1920]{1,0:T(8,128)S(1)}, u32[]{:S(2)}, u32[]{:S(2)}) %collective-permute-start.7) | collective-permute-done | bytes 122912 | tf_op jit(solution)/shard_map/ppermute | solution.py:417
  48.7 3.6 %collective-permute-done.6.refs_3_.below_ref = f32[16,1920]{1,0:T(8,128)S(1)} collective-permute-done((f32[16,1920]{1,0:T(8,128)S(1)}, f32[16,1920]{1,0:T(8,128)S(1)}, u32[]{:S(2)}, u32[]{:S(2)}) %collective-permute-start.6) | collective-permute-done | bytes 122912 | tf_op jit(solution)/shard_map/ppermute | solution.py:417
  52.3 0.3 shard_map.99.one_ref
  52.6 6.6 %collective-permute-start.8 = (f32[16,128]{1,0:T(8,128)S(1)}, f32[16,128]{1,0:T(8,128)S(1)}, u32[]{:S(2)}, u32[]{:S(2)}) collective-permute-start(f32[16,128]{1,0:T(8,128)S(1)} %shard_map.99.one_ref), channel_id=1, source_target_pairs={{0,8},{1,9},{2,10},{3,11},{4,12},{5,13},{6,14},{7,15},{8,0},{9,1},... | collective-permute-start | bytes 24584 | tf_op jit(solution)/shard_map/ppermute | solution.py:417
  59.2 0.0 copy-start.4
  59.2 2.2 %copy-done.4 = bf16[16,512,256]{2,1,0:T(8,128)(2,1)S(1)} copy-done((bf16[16,512,256]{2,1,0:T(8,128)(2,1)S(1)}, bf16[16,512,256]{2,1,0:T(8,128)(2,1)}, u32[]{:S(2)}) %copy-start.4) | copy-done | bytes 4194328
  61.4 1.3 %shard_map.100.start_ref = f32[16,4096]{1,0:T(8,128)S(1)} custom-call(f32[16,4736]{1,0:T(8,128)S(1)} %get-tuple-element.18.refs_0_.payload_ref.own_ref, bf16[16,512,256]{2,1,0:T(8,128)(2,1)S(1)} %copy-done.4), custom_call_target="tpu_custom_call" | custom-call | tf_op jit(solution)/shard_map/pallas_call | solution.py:381
  62.7 0.0 copy-done.12
  62.7 0.0 copy-start.2
  62.7 0.0 copy-start.7
  62.7 1.7 %shard_map.101.near_ref = f32[16,4096]{1,0:T(8,128)S(1)} custom-call(s32[1]{0:T(128)} %bitcast.1.base_ref, s32[4,16]{1,0:T(4,128)S(1)} %bitcast.4, f32[16,4736]{1,0:T(8,128)S(1)} %get-tuple-element.18.refs_0_.payload_ref.own_ref, f32[16,4736]{1,0:T(8,128)S(1)} %collective-permute-done.4.refs_1_.left_ref, ...), custom_call_target="tpu_custom_call" | custom-call | tf_op jit(solution)/shard_map/pallas_call | solution.py:381
  64.4 0.0 copy-done.2
  64.4 2.1 %shard_map.102.again_ref = f32[16,4096]{1,0:T(8,128)S(1)} custom-call(s32[16,32]{1,0:T(8,128)S(1)} %fusion.3.at_ref, f32[16,1920]{1,0:T(8,128)S(1)} %collective-permute-done.6.refs_3_.below_ref, f32[16,1920]{1,0:T(8,128)S(1)} %collective-permute-done.7.refs_4_.above_ref, bf16[16,64,1024]{2,1,0:T(8,128)(2,1)S(1)} %get-tuple-element.20.coupling_ref, ...), custom_call_target="tpu_custom_call" | custom-call | tf_op jit(solution)/shard_map/pallas_call | solution.py:381
  66.5 0.0 collective-permute-done.8.two_ref
  66.5 0.0 copy-done.7
  66.5 1.2 %shard_map.103 = (f32[16,4096]{1,0:T(8,128)}, f32[16,4096]{1,0:T(8,128)}) custom-call(f32[16,128]{1,0:T(8,128)S(1)} %shard_map.99.one_ref, f32[16,128]{1,0:T(8,128)S(1)} %collective-permute-done.8.two_ref, f32[16,4096]{1,0:T(8,128)S(1)} %copy-done.7, f32[16,4096]{1,0:T(8,128)S(1)} %get-tuple-element.19.image_ref, f32[16,4096]{1,0:T(8,128)S(1)} %shard_map.102.again_ref), custom_call_target="tpu_custom_call" | custom-call | tf_op jit(solution)/shard_map/pallas_call | solution.py:381
  (8 shorter events, 0.0 us)
Async XLA Ops:
  0.6 62.0 %copy-start.12 = (s32[16,4]{0,1:T(4,128)S(1)}, s32[16,4]{0,1:T(4,128)}, u32[]{:S(2)}) copy-start(s32[16,4]{0,1:T(4,128)} %param.10) | copy-start | bytes 772
  0.6 1.0 %copy-start = (f32[32,4096]{1,0:T(8,128)S(1)}, f32[32,4096]{1,0:T(8,128)}, u32[]{:S(2)}) copy-start(f32[32,4096]{1,0:T(8,128)} %basis_ref.3) | copy-start | bytes 1572868
  1.7 0.9 %copy-start.5 = (f32[16,4096]{1,0:T(8,128)S(1)}, f32[16,4096]{1,0:T(8,128)}, u32[]{:S(2)}) copy-start(f32[16,4096]{1,0:T(8,128)} %krylov_ref.3) | copy-start | bytes 786436
  2.6 0.8 %copy-start.8 = (s32[3,4096]{1,0:T(4,128)S(1)}, s32[3,4096]{1,0:T(4,128)}, u32[]{:S(2)}) copy-start(s32[3,4096]{1,0:T(4,128)} %corners_hbm.1) | copy-start | bytes 147460
  3.5 0.8 %copy-start.10 = (f32[3,2048]{1,0:T(4,128)S(1)}, f32[3,2048]{1,0:T(4,128)}, u32[]{:S(2)}) copy-start(f32[3,2048]{1,0:T(4,128)} %vertices_hbm.1) | copy-start | bytes 73732
  5.1 10.8 %collective-permute-start.1 = (f32[16,5632]{1,0:T(8,128)S(1)}, f32[16,5632]{1,0:T(8,128)S(1)}, u32[]{:S(2)}, u32[]{:S(2)}) collective-permute-start(f32[16,5632]{1,0:T(8,128)S(1)} %get-tuple-element.13.payload_ref.own_ref), channel_id=1, source_target_pairs={{0,15},{1,0},{2,1},{3,2},{4,3},{5,4},{6,5},{7,6},{8,7},{9,8},{10,9... | collective-permute-start | bytes 1081352 | tf_op jit(solution)/shard_map/ppermute | solution.py:417
  5.8 10.1 %collective-permute-start = (f32[16,5632]{1,0:T(8,128)S(1)}, f32[16,5632]{1,0:T(8,128)S(1)}, u32[]{:S(2)}, u32[]{:S(2)}) collective-permute-start(f32[16,5632]{1,0:T(8,128)S(1)} %get-tuple-element.13.payload_ref.own_ref), channel_id=1, source_target_pairs={{0,1},{1,2},{2,3},{3,4},{4,5},{5,6},{6,7},{7,8},{8,9},{9,10},{10,1... | collective-permute-start | bytes 1081352 | tf_op jit(solution)/shard_map/ppermute | solution.py:417
  10.2 2.0 %copy-start.3 = (bf16[16,512,256]{2,1,0:T(8,128)(2,1)}, bf16[16,512,256]{2,1,0:T(8,128)(2,1)S(1)}, u32[]{:S(2)}) copy-start(bf16[16,512,256]{2,1,0:T(8,128)(2,1)S(1)} %get-tuple-element.21.blocks_ref) | copy-start | bytes 12582916
  16.0 8.5 %collective-permute-start.3 = (f32[16,2304]{1,0:T(8,128)S(1)}, f32[16,2304]{1,0:T(8,128)S(1)}, u32[]{:S(2)}, u32[]{:S(2)}) collective-permute-start(f32[16,2304]{1,0:T(8,128)S(1)} %pad_maximum_fusion), channel_id=1, source_target_pairs={{0,13},{1,14},{2,15},{3,0},{4,1},{5,2},{6,3},{7,4},{8,5},{9,6},{10... | collective-permute-start | bytes 442376 | tf_op jit(solution)/shard_map/ppermute | solution.py:417
  17.7 7.1 %collective-permute-start.2 = (f32[16,2304]{1,0:T(8,128)S(1)}, f32[16,2304]{1,0:T(8,128)S(1)}, u32[]{:S(2)}, u32[]{:S(2)}) collective-permute-start(f32[16,2304]{1,0:T(8,128)S(1)} %pad_maximum_fusion), channel_id=1, source_target_pairs={{0,3},{1,4},{2,5},{3,6},{4,7},{5,8},{6,9},{7,10},{8,11},{9,12},{10... | collective-permute-start | bytes 442376 | tf_op jit(solution)/shard_map/ppermute | solution.py:417
  18.5 0.7 %copy-start.11 = (s32[16,4]{0,1:T(4,128)S(1)}, s32[16,4]{0,1:T(4,128)}, u32[]{:S(2)}) copy-start(s32[16,4]{0,1:T(4,128)} %param.10) | copy-start | bytes 772
  24.7 1.0 %copy-start.1 = (f32[32,4096]{1,0:T(8,128)S(1)}, f32[32,4096]{1,0:T(8,128)}, u32[]{:S(2)}) copy-start(f32[32,4096]{1,0:T(8,128)} %basis_ref.3) | copy-start | bytes 1572868
  25.8 0.9 %copy-start.6 = (f32[16,4096]{1,0:T(8,128)S(1)}, f32[16,4096]{1,0:T(8,128)}, u32[]{:S(2)}) copy-start(f32[16,4096]{1,0:T(8,128)} %krylov_ref.3) | copy-start | bytes 786436
  26.7 0.8 %copy-start.9 = (f32[3,32,128]{2,1,0:T(8,128)S(1)}, f32[3,32,128]{2,1,0:T(8,128)}, u32[]{:S(2)}) copy-start(f32[3,32,128]{2,1,0:T(8,128)} %constant.66.clone.upright_ref) | copy-start | bytes 147460
  27.5 0.7 %copy-start.13 = (f32[8,128]{1,0:T(8,128)S(1)}, f32[8,128]{1,0:T(8,128)}, u32[]{:S(2)}) copy-start(f32[8,128]{1,0:T(8,128)} %constant.67.clone.flat_ref) | copy-start | bytes 12292
  31.7 12.6 %collective-permute-start.5 = (f32[16,4736]{1,0:T(8,128)S(1)}, f32[16,4736]{1,0:T(8,128)S(1)}, u32[]{:S(2)}, u32[]{:S(2)}) collective-permute-start(f32[16,4736]{1,0:T(8,128)S(1)} %get-tuple-element.18.refs_0_.payload_ref.own_ref), channel_id=1, source_target_pairs={{0,15},{1,0},{2,1},{3,2},{4,3},{5,4},{6,5},{7,6},{8,7},{9,8},{10,9... | collective-permute-start | bytes 909320 | tf_op jit(solution)/shard_map/ppermute | solution.py:417
  31.7 12.6 %collective-permute-start.4 = (f32[16,4736]{1,0:T(8,128)S(1)}, f32[16,4736]{1,0:T(8,128)S(1)}, u32[]{:S(2)}, u32[]{:S(2)}) collective-permute-start(f32[16,4736]{1,0:T(8,128)S(1)} %get-tuple-element.18.refs_0_.payload_ref.own_ref), channel_id=1, source_target_pairs={{0,1},{1,2},{2,3},{3,4},{4,5},{5,6},{6,7},{7,8},{8,9},{9,10},{10,1... | collective-permute-start | bytes 909320 | tf_op jit(solution)/shard_map/ppermute | solution.py:417
  44.3 4.4 %collective-permute-start.7 = (f32[16,1920]{1,0:T(8,128)S(1)}, f32[16,1920]{1,0:T(8,128)S(1)}, u32[]{:S(2)}, u32[]{:S(2)}) collective-permute-start(f32[16,1920]{1,0:T(8,128)S(1)} %pad_maximum_fusion.1), channel_id=1, source_target_pairs={{0,13},{1,14},{2,15},{3,0},{4,1},{5,2},{6,3},{7,4},{8,5},{9,6},{10... | collective-permute-start | bytes 368648 | tf_op jit(solution)/shard_map/ppermute | solution.py:417
  44.4 7.9 %collective-permute-start.6 = (f32[16,1920]{1,0:T(8,128)S(1)}, f32[16,1920]{1,0:T(8,128)S(1)}, u32[]{:S(2)}, u32[]{:S(2)}) collective-permute-start(f32[16,1920]{1,0:T(8,128)S(1)} %pad_maximum_fusion.1), channel_id=1, source_target_pairs={{0,3},{1,4},{2,5},{3,6},{4,7},{5,8},{6,9},{7,10},{8,11},{9,12},{10... | collective-permute-start | bytes 368648 | tf_op jit(solution)/shard_map/ppermute | solution.py:417
  52.6 13.9 %collective-permute-start.8 = (f32[16,128]{1,0:T(8,128)S(1)}, f32[16,128]{1,0:T(8,128)S(1)}, u32[]{:S(2)}, u32[]{:S(2)}) collective-permute-start(f32[16,128]{1,0:T(8,128)S(1)} %shard_map.99.one_ref), channel_id=1, source_target_pairs={{0,8},{1,9},{2,10},{3,11},{4,12},{5,13},{6,14},{7,15},{8,0},{9,1},... | collective-permute-start | bytes 24584 | tf_op jit(solution)/shard_map/ppermute | solution.py:417
  59.2 2.2 %copy-start.4 = (bf16[16,512,256]{2,1,0:T(8,128)(2,1)S(1)}, bf16[16,512,256]{2,1,0:T(8,128)(2,1)}, u32[]{:S(2)}) copy-start(bf16[16,512,256]{2,1,0:T(8,128)(2,1)} %copy-done.3) | copy-start | bytes 12582916
  62.7 1.7 %copy-start.2 = (f32[32,4096]{1,0:T(8,128)S(1)}, f32[32,4096]{1,0:T(8,128)}, u32[]{:S(2)}) copy-start(f32[32,4096]{1,0:T(8,128)} %basis_ref.3) | copy-start | bytes 1572868
  62.7 3.8 %copy-start.7 = (f32[16,4096]{1,0:T(8,128)S(1)}, f32[16,4096]{1,0:T(8,128)}, u32[]{:S(2)}) copy-start(f32[16,4096]{1,0:T(8,128)} %krylov_ref.3) | copy-start | bytes 786436
